TPU v7x, 256 devices: a whole 4x4x8 slice. The times are simulated.
256 devices in a mesh: gy: 16 (over z, core), gx: 16 (over y, x).
Axes of the slice: x: 4, y: 4, z: 8, core: 2. Of those that a mesh axis runs over, the one named last changes fastest.
Arguments:
- embedding: bfloat16 [16, 6, 1024, 4096], P(None, None, 'gy', 'gx'), may hold values from -4 to 4
- offsets: int32 [12, 3], replicated, may hold values from -27 to 27, as said below
- targets: int32 [6, 1024, 4096], P(None, 'gy', 'gx'), may hold values from 0 to 4095
- mask: int32 [6, 1024, 4096], P(None, 'gy', 'gx'), may hold values 0 or 1
Outputs:
- embed_grad: float32 [16, 6, 1024, 4096], P(None, None, 'gy', 'gx')
Inputs may be any that keep to these rules, and one draw needn't show every extreme that they name: `offsets`: each row is (z, y, x) with |z| <= 3 and |y|, |x| <= 27, never all zero; row 0 has y = 27, row 1 has x = -27, row 2 has z = 3.
All inputs are finite; a program needn't handle non-finite values. No bound on the sum of `mask` on one device may be relied on, other than what follows from the above.
Results may differ from a plain program's by a relative error of at most 0.0006.
Values may be sent and summed in bfloat16 or wider, within the bound.
A program may use at most 192 MiB of HBM per device.

v0:
```python
import jax
import jax.numpy as jnp
from jax import lax
from jax.sharding import PartitionSpec as P

K = 12
REACH = 27
ZR = 3


def with_halo(cells, sides, width):
    for axis, dim in sides:
        count = lax.axis_size(axis)
        ends = count - 1
        head = lax.slice_in_dim(cells, 0, width, axis=dim)
        tail = lax.slice_in_dim(cells, cells.shape[dim] - width, cells.shape[dim], axis=dim)
        cells = jnp.concatenate(
            [
                lax.ppermute(tail, axis, [(i, (i + 1) % count) for i in range(ends)]),
                cells,
                lax.ppermute(head, axis, [((i + 1) % count, i) for i in range(ends)]),
            ],
            axis=dim,
        )
    return cells


def window(extended, shift_z, shift_y, shift_x, shape):
    anchor = (jnp.int32(0), ZR + shift_z, REACH + shift_y, REACH + shift_x)
    return lax.dynamic_slice(extended, anchor, shape)


def on_device(embedding, offsets, targets, mask):
    channels, slices, row_count, col_count = embedding.shape
    span_y = row_count * lax.axis_size("gy")
    span_x = col_count * lax.axis_size("gx")
    z_index = jnp.arange(slices, dtype=jnp.int32)[:, None, None]
    y_index = (lax.axis_index("gy") * row_count + jnp.arange(row_count, dtype=jnp.int32))[
        None, :, None
    ]
    x_index = (lax.axis_index("gx") * col_count + jnp.arange(col_count, dtype=jnp.int32))[
        None, None, :
    ]
    block_shape = (channels, slices, row_count, col_count)
    extended = with_halo(embedding, (("gy", 2), ("gx", 3)), REACH)
    extended = jnp.pad(extended, ((0, 0), (ZR, ZR), (0, 0), (0, 0)))
    keep_mask = mask.astype(jnp.float32)

    def inside_of(shift_z, shift_y, shift_x):
        inside = (
            (z_index + shift_z >= 0)
            & (z_index + shift_z < slices)
            & (y_index + shift_y >= 0)
            & (y_index + shift_y < span_y)
            & (x_index + shift_x >= 0)
            & (x_index + shift_x < span_x)
        )
        return inside.astype(jnp.float32)

    def offset_of(which):
        which = which.astype(jnp.int32)
        return (which, offsets[which, 0], offsets[which, 1], offsets[which, 2])

    def slope_of(which, own_float, partner, labels, keep_here, inside):
        logits = jnp.sum(own_float * partner, axis=0)
        target_bit = jnp.bitwise_and(jnp.right_shift(labels, which), 1).astype(jnp.float32)
        return keep_here * inside * (jax.nn.sigmoid(logits) - target_bit)

    own_float = embedding.astype(jnp.float32)
    own_grad = jnp.zeros(block_shape, jnp.float32)

    def forward_step(own_acc, which):
        which, shift_z, shift_y, shift_x = offset_of(which)
        partner = window(extended, shift_z, shift_y, shift_x, block_shape).astype(jnp.float32)
        slope = slope_of(
            which, own_float, partner, targets, keep_mask, inside_of(shift_z, shift_y, shift_x)
        )
        return (own_acc + slope[None] * partner, slope)

    own_grad, slopes = lax.scan(forward_step, own_grad, jnp.arange(K, dtype=jnp.int32))
    slope_wide = with_halo(slopes, (("gy", 2), ("gx", 3)), REACH)
    slope_wide = jnp.pad(slope_wide, ((0, 0), (ZR, ZR), (0, 0), (0, 0)))

    def return_step(which, own_acc):
        which, shift_z, shift_y, shift_x = offset_of(which)
        anchor = (which, ZR - shift_z, REACH - shift_y, REACH - shift_x)
        slope = lax.dynamic_slice(slope_wide, anchor, (1, slices, row_count, col_count))
        source = window(extended, -shift_z, -shift_y, -shift_x, block_shape).astype(jnp.float32)
        return own_acc + slope * source

    return lax.fori_loop(0, K, return_step, own_grad)


def solution(mesh):
    return jax.shard_map(
        on_device,
        mesh=mesh,
        in_specs=(P(None, None, "gy", "gx"), P(), P(None, "gy", "gx"), P(None, "gy", "gx")),
        out_specs=P(None, None, "gy", "gx"),
        check_vma=False,
    )
```

profile of v0, /device:TPU:71, one launch (start us, length us, event | category | flops | bytes accessed | tf_op | source)
XLA Modules:
  0.0 799.8 jit_solution(17049367109065444570)
XLA Ops:
  4.8 4.1 collective-permute-start
  12.7 6.7 copy.19
  19.4 4.5 collective-permute-done
  24.0 8.3 %copy.18 = bf16[16,6,27,256]{2,0,3,1:T(8,128)(2,1)} copy(bf16[16,6,27,256]{3,0,2,1:T(8,128)(2,1)} %collective-permute-done) | data formatting | bytes 2654208 | tf_op jit(solution)/shard_map/ppermute | solution.py:19
  32.3 8.4 %copy.20 = bf16[16,6,27,256]{2,0,3,1:T(8,128)(2,1)} copy(bf16[16,6,27,256]{3,0,2,1:T(8,128)(2,1)} %collective-permute-done.1) | data formatting | bytes 2654208 | tf_op jit(solution)/shard_map/ppermute | solution.py:21
  40.7 4.5 pad_maximum_fusion.7
  45.2 3.2 collective-permute-start.2
  50.8 3.5 convert_element_type.48
  54.3 8.6 %collective-permute-done.2 = bf16[16,6,118,27]{2,0,3,1:T(8,128)(2,1)} collective-permute-done((bf16[16,6,118,27]{2,0,3,1:T(8,128)(2,1)}, bf16[16,6,118,27]{2,0,3,1:T(8,128)(2,1)}, u32[]{:S(2)}, u32[]{:S(2)}) %collective-permute-start.2) | collective-permute-done | bytes 611744 | tf_op jit(solution)/shard_map/ppermute | solution.py:19
  62.9 4.9 collective-permute-done.3
  67.9 12.3 %pad_maximum_fusion.1 = bf16[16,6,118,310]{2,0,3,1:T(8,128)(2,1)} fusion(bf16[16,6,118,27]{2,0,3,1:T(8,128)(2,1)} %collective-permute-done.3, bf16[16,6,27,256]{2,0,3,1:T(8,128)(2,1)} %copy.20, bf16[16,6,64,256]{2,0,3,1:T(8,128)(2,1)} %copy.19, bf16[16,6,27,256]{2,0,3,1:T(8,128)(2,1)} %copy.18, bf16[16,6,118,27]{2,0,3,1:T(8,128)(2,1)} %collective-permute-done.2), kind=kLoop, calls=%fused_computation.30 | loop fusion | flops 35116800 | bytes 14046720 | tf_op jit(solution)/shard_map/concatenate | solution.py:17
  80.2 12.3 %copy.29 = bf16[16,6,118,310]{3,2,1,0:T(8,128)(2,1)} copy(bf16[16,6,118,310]{2,0,3,1:T(8,128)(2,1)} %pad_maximum_fusion.1) | data formatting | bytes 14046720
  92.4 10.6 %pad.8.clone = bf16[16,12,118,310]{3,2,1,0:T(8,128)(2,1)} pad(bf16[16,6,118,310]{3,2,1,0:T(8,128)(2,1)} %copy.29, bf16[]{:T(256)} %constant.200.clone.1), padding=0_0x3_3x0_0x0_0 | pad | bytes 21070082 | tf_op jit(solution)/shard_map/jit(_pad)/pad | solution.py:46
  103.0 347.6 %while.32 = (s32[]{:T(128)}, f32[16,6,64,256]{3,2,1,0:T(8,128)}, f32[12,6,64,256]{3,2,1,0:T(8,128)}, s32[12]{0:T(128)S(1)}, s32[12,3]{0,1:T(4,128)S(1)}, /*index...) while((s32[]{:T(128)}, f32[16,6,64,256]{3,2,1,0:T(8,128)}, ...), condition=%wide.region_2.3_spmd.clone, body=%wide.region_0.2_spmd.clone.sunk | while | flops 13076522 | bytes 29102408 | solution.py:80
  109.7 7.5 fusion.14
  119.9 8.9 %fusion.15 = f32[16,6,64,256]{3,2,1,0:T(8,128)} fusion(f32[16,6,64,256]{3,2,1,0:T(8,128)} %get-tuple-element.584, f32[6,64,256]{2,1,0:T(8,128)S(1)} %select_multiply_fusion.2, pred[]{:T(512)S(6)} %compare.5, bf16[16,12,118,310]{3,2,1,0:T(8,128)(2,1)} %get-tuple-element.608, s32[]{:T(128)S(6)} %select_n.125, s32[]{:T(128)S(6)} %select_n.126, ...), kind=kLoop, calls=%fused_computation.11.clone.1 | loop fusion | flops 6291456 | bytes 16121869 | tf_op jit(solution)/shard_map/while/body/eval_jaxpr/add | solution.py:78
  137.0 7.5 fusion.14
  147.3 10.7 %fusion.15 = f32[16,6,64,256]{3,2,1,0:T(8,128)} fusion(f32[16,6,64,256]{3,2,1,0:T(8,128)} %get-tuple-element.584, f32[6,64,256]{2,1,0:T(8,128)S(1)} %select_multiply_fusion.2, pred[]{:T(512)S(6)} %compare.5, bf16[16,12,118,310]{3,2,1,0:T(8,128)(2,1)} %get-tuple-element.608, s32[]{:T(128)S(6)} %select_n.125, s32[]{:T(128)S(6)} %select_n.126, ...), kind=kLoop, calls=%fused_computation.11.clone.1 | loop fusion | flops 6291456 | bytes 16121869 | tf_op jit(solution)/shard_map/while/body/eval_jaxpr/add | solution.py:78
  166.1 7.5 fusion.14
  176.4 10.7 %fusion.15 = f32[16,6,64,256]{3,2,1,0:T(8,128)} fusion(f32[16,6,64,256]{3,2,1,0:T(8,128)} %get-tuple-element.584, f32[6,64,256]{2,1,0:T(8,128)S(1)} %select_multiply_fusion.2, pred[]{:T(512)S(6)} %compare.5, bf16[16,12,118,310]{3,2,1,0:T(8,128)(2,1)} %get-tuple-element.608, s32[]{:T(128)S(6)} %select_n.125, s32[]{:T(128)S(6)} %select_n.126, ...), kind=kLoop, calls=%fused_computation.11.clone.1 | loop fusion | flops 6291456 | bytes 16121869 | tf_op jit(solution)/shard_map/while/body/eval_jaxpr/add | solution.py:78
  195.2 7.5 fusion.14
  205.5 10.7 %fusion.15 = f32[16,6,64,256]{3,2,1,0:T(8,128)} fusion(f32[16,6,64,256]{3,2,1,0:T(8,128)} %get-tuple-element.584, f32[6,64,256]{2,1,0:T(8,128)S(1)} %select_multiply_fusion.2, pred[]{:T(512)S(6)} %compare.5, bf16[16,12,118,310]{3,2,1,0:T(8,128)(2,1)} %get-tuple-element.608, s32[]{:T(128)S(6)} %select_n.125, s32[]{:T(128)S(6)} %select_n.126, ...), kind=kLoop, calls=%fused_computation.11.clone.1 | loop fusion | flops 6291456 | bytes 16121869 | tf_op jit(solution)/shard_map/while/body/eval_jaxpr/add | solution.py:78
  224.3 7.5 fusion.14
  234.6 10.7 %fusion.15 = f32[16,6,64,256]{3,2,1,0:T(8,128)} fusion(f32[16,6,64,256]{3,2,1,0:T(8,128)} %get-tuple-element.584, f32[6,64,256]{2,1,0:T(8,128)S(1)} %select_multiply_fusion.2, pred[]{:T(512)S(6)} %compare.5, bf16[16,12,118,310]{3,2,1,0:T(8,128)(2,1)} %get-tuple-element.608, s32[]{:T(128)S(6)} %select_n.125, s32[]{:T(128)S(6)} %select_n.126, ...), kind=kLoop, calls=%fused_computation.11.clone.1 | loop fusion | flops 6291456 | bytes 16121869 | tf_op jit(solution)/shard_map/while/body/eval_jaxpr/add | solution.py:78
  253.4 7.5 fusion.14
  263.7 10.7 %fusion.15 = f32[16,6,64,256]{3,2,1,0:T(8,128)} fusion(f32[16,6,64,256]{3,2,1,0:T(8,128)} %get-tuple-element.584, f32[6,64,256]{2,1,0:T(8,128)S(1)} %select_multiply_fusion.2, pred[]{:T(512)S(6)} %compare.5, bf16[16,12,118,310]{3,2,1,0:T(8,128)(2,1)} %get-tuple-element.608, s32[]{:T(128)S(6)} %select_n.125, s32[]{:T(128)S(6)} %select_n.126, ...), kind=kLoop, calls=%fused_computation.11.clone.1 | loop fusion | flops 6291456 | bytes 16121869 | tf_op jit(solution)/shard_map/while/body/eval_jaxpr/add | solution.py:78
  282.5 7.5 fusion.14
  292.8 10.7 %fusion.15 = f32[16,6,64,256]{3,2,1,0:T(8,128)} fusion(f32[16,6,64,256]{3,2,1,0:T(8,128)} %get-tuple-element.584, f32[6,64,256]{2,1,0:T(8,128)S(1)} %select_multiply_fusion.2, pred[]{:T(512)S(6)} %compare.5, bf16[16,12,118,310]{3,2,1,0:T(8,128)(2,1)} %get-tuple-element.608, s32[]{:T(128)S(6)} %select_n.125, s32[]{:T(128)S(6)} %select_n.126, ...), kind=kLoop, calls=%fused_computation.11.clone.1 | loop fusion | flops 6291456 | bytes 16121869 | tf_op jit(solution)/shard_map/while/body/eval_jaxpr/add | solution.py:78
  311.6 7.5 fusion.14
  321.9 10.7 %fusion.15 = f32[16,6,64,256]{3,2,1,0:T(8,128)} fusion(f32[16,6,64,256]{3,2,1,0:T(8,128)} %get-tuple-element.584, f32[6,64,256]{2,1,0:T(8,128)S(1)} %select_multiply_fusion.2, pred[]{:T(512)S(6)} %compare.5, bf16[16,12,118,310]{3,2,1,0:T(8,128)(2,1)} %get-tuple-element.608, s32[]{:T(128)S(6)} %select_n.125, s32[]{:T(128)S(6)} %select_n.126, ...), kind=kLoop, calls=%fused_computation.11.clone.1 | loop fusion | flops 6291456 | bytes 16121869 | tf_op jit(solution)/shard_map/while/body/eval_jaxpr/add | solution.py:78
  340.8 7.5 fusion.14
  351.1 10.7 %fusion.15 = f32[16,6,64,256]{3,2,1,0:T(8,128)} fusion(f32[16,6,64,256]{3,2,1,0:T(8,128)} %get-tuple-element.584, f32[6,64,256]{2,1,0:T(8,128)S(1)} %select_multiply_fusion.2, pred[]{:T(512)S(6)} %compare.5, bf16[16,12,118,310]{3,2,1,0:T(8,128)(2,1)} %get-tuple-element.608, s32[]{:T(128)S(6)} %select_n.125, s32[]{:T(128)S(6)} %select_n.126, ...), kind=kLoop, calls=%fused_computation.11.clone.1 | loop fusion | flops 6291456 | bytes 16121869 | tf_op jit(solution)/shard_map/while/body/eval_jaxpr/add | solution.py:78
  369.9 7.5 fusion.14
  380.2 10.7 %fusion.15 = f32[16,6,64,256]{3,2,1,0:T(8,128)} fusion(f32[16,6,64,256]{3,2,1,0:T(8,128)} %get-tuple-element.584, f32[6,64,256]{2,1,0:T(8,128)S(1)} %select_multiply_fusion.2, pred[]{:T(512)S(6)} %compare.5, bf16[16,12,118,310]{3,2,1,0:T(8,128)(2,1)} %get-tuple-element.608, s32[]{:T(128)S(6)} %select_n.125, s32[]{:T(128)S(6)} %select_n.126, ...), kind=kLoop, calls=%fused_computation.11.clone.1 | loop fusion | flops 6291456 | bytes 16121869 | tf_op jit(solution)/shard_map/while/body/eval_jaxpr/add | solution.py:78
  399.0 7.5 fusion.14
  409.3 10.7 %fusion.15 = f32[16,6,64,256]{3,2,1,0:T(8,128)} fusion(f32[16,6,64,256]{3,2,1,0:T(8,128)} %get-tuple-element.584, f32[6,64,256]{2,1,0:T(8,128)S(1)} %select_multiply_fusion.2, pred[]{:T(512)S(6)} %compare.5, bf16[16,12,118,310]{3,2,1,0:T(8,128)(2,1)} %get-tuple-element.608, s32[]{:T(128)S(6)} %select_n.125, s32[]{:T(128)S(6)} %select_n.126, ...), kind=kLoop, calls=%fused_computation.11.clone.1 | loop fusion | flops 6291456 | bytes 16121869 | tf_op jit(solution)/shard_map/while/body/eval_jaxpr/add | solution.py:78
  428.1 7.5 fusion.14
  438.4 10.7 %fusion.15 = f32[16,6,64,256]{3,2,1,0:T(8,128)} fusion(f32[16,6,64,256]{3,2,1,0:T(8,128)} %get-tuple-element.584, f32[6,64,256]{2,1,0:T(8,128)S(1)} %select_multiply_fusion.2, pred[]{:T(512)S(6)} %compare.5, bf16[16,12,118,310]{3,2,1,0:T(8,128)(2,1)} %get-tuple-element.608, s32[]{:T(128)S(6)} %select_n.125, s32[]{:T(128)S(6)} %select_n.126, ...), kind=kLoop, calls=%fused_computation.11.clone.1 | loop fusion | flops 6291456 | bytes 16121869 | tf_op jit(solution)/shard_map/while/body/eval_jaxpr/add | solution.py:78
  450.6 4.5 fusion.9
  455.1 6.8 collective-permute-start.4
  464.1 8.0 %copy.23 = f32[12,6,64,256]{2,3,1,0:T(8,128)} copy(f32[12,6,64,256]{3,2,1,0:T(8,128)} %get-tuple-element.318) | data formatting | bytes 9437184 | tf_op jit(solution)/shard_map/while | solution.py:80
  472.1 15.9 %collective-permute-done.4 = f32[12,6,27,256]{3,2,1,0:T(8,128)} collective-permute-done((f32[12,6,27,256]{3,2,1,0:T(8,128)}, f32[12,6,27,256]{3,2,1,0:T(8,128)}, u32[]{:S(2)}, u32[]{:S(2)}) %collective-permute-start.4) | collective-permute-done | bytes 1990688 | tf_op jit(solution)/shard_map/ppermute | solution.py:19
  488.0 6.7 copy.22
  494.8 6.7 copy.24
  501.5 5.4 pad_maximum_fusion.4
  508.8 3.4 collective-permute-start.7
  512.1 24.6 %collective-permute-done.6 = f32[12,6,118,27]{2,3,1,0:T(8,128)S(1)} collective-permute-done((f32[12,6,118,27]{2,3,1,0:T(8,128)}, f32[12,6,118,27]{2,3,1,0:T(8,128)S(1)}, u32[]{:S(2)}, u32[]{:S(2)}) %collective-permute-start.6) | collective-permute-done | bytes 917600 | tf_op jit(solution)/shard_map/ppermute | solution.py:19
  536.7 3.8 collective-permute-done.7
  540.6 16.0 %pad_maximum_fusion = f32[12,6,118,310]{2,3,1,0:T(8,128)} fusion(f32[12,6,118,27]{2,3,1,0:T(8,128)S(1)} %collective-permute-done.7, f32[12,6,27,256]{2,3,1,0:T(8,128)} %copy.24, f32[12,6,64,256]{2,3,1,0:T(8,128)} %copy.23, f32[12,6,27,256]{2,3,1,0:T(8,128)} %copy.22, f32[12,6,118,27]{2,3,1,0:T(8,128)S(1)} %collective-permute-done.6), kind=kLoop, calls=%fused_computation.29 | loop fusion | flops 10535040 | bytes 21070080 | tf_op jit(solution)/shard_map/concatenate | solution.py:17
  556.6 12.7 %copy.30 = f32[12,6,118,310]{3,2,1,0:T(8,128)} copy(f32[12,6,118,310]{2,3,1,0:T(8,128)} %pad_maximum_fusion) | data formatting | bytes 21070080
  569.3 14.5 %pad.9.clone = f32[12,12,118,310]{3,2,1,0:T(8,128)} pad(f32[12,6,118,310]{3,2,1,0:T(8,128)} %copy.30, f32[]{:T(128)} %constant.199.clone.1), padding=0_0x3_3x0_0x0_0 | pad | bytes 31605124 | tf_op jit(solution)/shard_map/jit(_pad)/pad | solution.py:82
  583.9 215.9 %while.31 = (s32[]{:T(128)}, f32[16,6,64,256]{3,2,1,0:T(8,128)}, s32[12,3]{0,1:T(4,128)S(1)}, f32[12,12,118,310]{3,2,1,0:T(8,128)}, bf16[16,12,118,310]{3,2,1,0:...) while((s32[]{:T(128)}, f32[16,6,64,256]{3,2,1,0:T(8,128)}, ...), condition=%wide.region_4.5_spmd, body=%wide.region_3.4_spmd.sunk | while | flops 4718621 | bytes 16908760 | solution.py:91
  591.5 10.4 %multiply_add_fusion.2 = f32[16,6,64,256]{3,2,1,0:T(8,128)} fusion(f32[16,6,64,256]{3,2,1,0:T(8,128)} %get-tuple-element.634, bf16[16,12,118,310]{3,2,1,0:T(8,128)(2,1)} %get-tuple-element.649, s32[]{:T(128)S(6)} %select_n.118, s32[]{:T(128)S(6)} %select_n.119, s32[]{:T(128)S(6)} %select_n.120, f32[6,64,256]{2,1,0:T(8,128)S(1)} %dynamic-slice_bitcast_fusion.2), kind=kLoop, calls=%fused_computation.3.clone.1 | loop fusion | flops 4718592 | bytes 16121868 | tf_op jit(solution)/shard_map/while/body/eval_jaxpr/add | solution.py:89
  609.5 10.4 %multiply_add_fusion.2 = f32[16,6,64,256]{3,2,1,0:T(8,128)} fusion(f32[16,6,64,256]{3,2,1,0:T(8,128)} %get-tuple-element.634, bf16[16,12,118,310]{3,2,1,0:T(8,128)(2,1)} %get-tuple-element.649, s32[]{:T(128)S(6)} %select_n.118, s32[]{:T(128)S(6)} %select_n.119, s32[]{:T(128)S(6)} %select_n.120, f32[6,64,256]{2,1,0:T(8,128)S(1)} %dynamic-slice_bitcast_fusion.2), kind=kLoop, calls=%fused_computation.3.clone.1 | loop fusion | flops 4718592 | bytes 16121868 | tf_op jit(solution)/shard_map/while/body/eval_jaxpr/add | solution.py:89
  627.5 10.4 %multiply_add_fusion.2 = f32[16,6,64,256]{3,2,1,0:T(8,128)} fusion(f32[16,6,64,256]{3,2,1,0:T(8,128)} %get-tuple-element.634, bf16[16,12,118,310]{3,2,1,0:T(8,128)(2,1)} %get-tuple-element.649, s32[]{:T(128)S(6)} %select_n.118, s32[]{:T(128)S(6)} %select_n.119, s32[]{:T(128)S(6)} %select_n.120, f32[6,64,256]{2,1,0:T(8,128)S(1)} %dynamic-slice_bitcast_fusion.2), kind=kLoop, calls=%fused_computation.3.clone.1 | loop fusion | flops 4718592 | bytes 16121868 | tf_op jit(solution)/shard_map/while/body/eval_jaxpr/add | solution.py:89
  645.5 10.4 %multiply_add_fusion.2 = f32[16,6,64,256]{3,2,1,0:T(8,128)} fusion(f32[16,6,64,256]{3,2,1,0:T(8,128)} %get-tuple-element.634, bf16[16,12,118,310]{3,2,1,0:T(8,128)(2,1)} %get-tuple-element.649, s32[]{:T(128)S(6)} %select_n.118, s32[]{:T(128)S(6)} %select_n.119, s32[]{:T(128)S(6)} %select_n.120, f32[6,64,256]{2,1,0:T(8,128)S(1)} %dynamic-slice_bitcast_fusion.2), kind=kLoop, calls=%fused_computation.3.clone.1 | loop fusion | flops 4718592 | bytes 16121868 | tf_op jit(solution)/shard_map/while/body/eval_jaxpr/add | solution.py:89
  663.5 10.4 %multiply_add_fusion.2 = f32[16,6,64,256]{3,2,1,0:T(8,128)} fusion(f32[16,6,64,256]{3,2,1,0:T(8,128)} %get-tuple-element.634, bf16[16,12,118,310]{3,2,1,0:T(8,128)(2,1)} %get-tuple-element.649, s32[]{:T(128)S(6)} %select_n.118, s32[]{:T(128)S(6)} %select_n.119, s32[]{:T(128)S(6)} %select_n.120, f32[6,64,256]{2,1,0:T(8,128)S(1)} %dynamic-slice_bitcast_fusion.2), kind=kLoop, calls=%fused_computation.3.clone.1 | loop fusion | flops 4718592 | bytes 16121868 | tf_op jit(solution)/shard_map/while/body/eval_jaxpr/add | solution.py:89
  681.5 10.4 %multiply_add_fusion.2 = f32[16,6,64,256]{3,2,1,0:T(8,128)} fusion(f32[16,6,64,256]{3,2,1,0:T(8,128)} %get-tuple-element.634, bf16[16,12,118,310]{3,2,1,0:T(8,128)(2,1)} %get-tuple-element.649, s32[]{:T(128)S(6)} %select_n.118, s32[]{:T(128)S(6)} %select_n.119, s32[]{:T(128)S(6)} %select_n.120, f32[6,64,256]{2,1,0:T(8,128)S(1)} %dynamic-slice_bitcast_fusion.2), kind=kLoop, calls=%fused_computation.3.clone.1 | loop fusion | flops 4718592 | bytes 16121868 | tf_op jit(solution)/shard_map/while/body/eval_jaxpr/add | solution.py:89
  699.5 10.4 %multiply_add_fusion.2 = f32[16,6,64,256]{3,2,1,0:T(8,128)} fusion(f32[16,6,64,256]{3,2,1,0:T(8,128)} %get-tuple-element.634, bf16[16,12,118,310]{3,2,1,0:T(8,128)(2,1)} %get-tuple-element.649, s32[]{:T(128)S(6)} %select_n.118, s32[]{:T(128)S(6)} %select_n.119, s32[]{:T(128)S(6)} %select_n.120, f32[6,64,256]{2,1,0:T(8,128)S(1)} %dynamic-slice_bitcast_fusion.2), kind=kLoop, calls=%fused_computation.3.clone.1 | loop fusion | flops 4718592 | bytes 16121868 | tf_op jit(solution)/shard_map/while/body/eval_jaxpr/add | solution.py:89
  717.4 10.4 %multiply_add_fusion.2 = f32[16,6,64,256]{3,2,1,0:T(8,128)} fusion(f32[16,6,64,256]{3,2,1,0:T(8,128)} %get-tuple-element.634, bf16[16,12,118,310]{3,2,1,0:T(8,128)(2,1)} %get-tuple-element.649, s32[]{:T(128)S(6)} %select_n.118, s32[]{:T(128)S(6)} %select_n.119, s32[]{:T(128)S(6)} %select_n.120, f32[6,64,256]{2,1,0:T(8,128)S(1)} %dynamic-slice_bitcast_fusion.2), kind=kLoop, calls=%fused_computation.3.clone.1 | loop fusion | flops 4718592 | bytes 16121868 | tf_op jit(solution)/shard_map/while/body/eval_jaxpr/add | solution.py:89
  735.4 10.4 %multiply_add_fusion.2 = f32[16,6,64,256]{3,2,1,0:T(8,128)} fusion(f32[16,6,64,256]{3,2,1,0:T(8,128)} %get-tuple-element.634, bf16[16,12,118,310]{3,2,1,0:T(8,128)(2,1)} %get-tuple-element.649, s32[]{:T(128)S(6)} %select_n.118, s32[]{:T(128)S(6)} %select_n.119, s32[]{:T(128)S(6)} %select_n.120, f32[6,64,256]{2,1,0:T(8,128)S(1)} %dynamic-slice_bitcast_fusion.2), kind=kLoop, calls=%fused_computation.3.clone.1 | loop fusion | flops 4718592 | bytes 16121868 | tf_op jit(solution)/shard_map/while/body/eval_jaxpr/add | solution.py:89
  753.4 10.4 %multiply_add_fusion.2 = f32[16,6,64,256]{3,2,1,0:T(8,128)} fusion(f32[16,6,64,256]{3,2,1,0:T(8,128)} %get-tuple-element.634, bf16[16,12,118,310]{3,2,1,0:T(8,128)(2,1)} %get-tuple-element.649, s32[]{:T(128)S(6)} %select_n.118, s32[]{:T(128)S(6)} %select_n.119, s32[]{:T(128)S(6)} %select_n.120, f32[6,64,256]{2,1,0:T(8,128)S(1)} %dynamic-slice_bitcast_fusion.2), kind=kLoop, calls=%fused_computation.3.clone.1 | loop fusion | flops 4718592 | bytes 16121868 | tf_op jit(solution)/shard_map/while/body/eval_jaxpr/add | solution.py:89
  771.4 10.4 %multiply_add_fusion.2 = f32[16,6,64,256]{3,2,1,0:T(8,128)} fusion(f32[16,6,64,256]{3,2,1,0:T(8,128)} %get-tuple-element.634, bf16[16,12,118,310]{3,2,1,0:T(8,128)(2,1)} %get-tuple-element.649, s32[]{:T(128)S(6)} %select_n.118, s32[]{:T(128)S(6)} %select_n.119, s32[]{:T(128)S(6)} %select_n.120, f32[6,64,256]{2,1,0:T(8,128)S(1)} %dynamic-slice_bitcast_fusion.2), kind=kLoop, calls=%fused_computation.3.clone.1 | loop fusion | flops 4718592 | bytes 16121868 | tf_op jit(solution)/shard_map/while/body/eval_jaxpr/add | solution.py:89
  789.4 10.4 %multiply_add_fusion.2 = f32[16,6,64,256]{3,2,1,0:T(8,128)} fusion(f32[16,6,64,256]{3,2,1,0:T(8,128)} %get-tuple-element.634, bf16[16,12,118,310]{3,2,1,0:T(8,128)(2,1)} %get-tuple-element.649, s32[]{:T(128)S(6)} %select_n.118, s32[]{:T(128)S(6)} %select_n.119, s32[]{:T(128)S(6)} %select_n.120, f32[6,64,256]{2,1,0:T(8,128)S(1)} %dynamic-slice_bitcast_fusion.2), kind=kLoop, calls=%fused_computation.3.clone.1 | loop fusion | flops 4718592 | bytes 16121868 | tf_op jit(solution)/shard_map/while/body/eval_jaxpr/add | solution.py:89
  (141 shorter events, 103.2 us)
Async XLA Ops:
  0.0 12.7 %copy-start.1 = (bf16[16,6,64,256]{3,2,1,0:T(8,128)(2,1)S(1)}, bf16[16,6,64,256]{3,2,1,0:T(8,128)(2,1)}, u32[]{:S(2)}) copy-start(bf16[16,6,64,256]{3,2,1,0:T(8,128)(2,1)} %param.8) | copy-start | bytes 9437188
  4.8 19.1 %collective-permute-start = (bf16[16,6,27,256]{3,0,2,1:T(8,128)(2,1)}, bf16[16,6,27,256]{3,0,2,1:T(8,128)(2,1)}, u32[]{:S(2)}, u32[]{:S(2)}) collective-permute-start(bf16[16,6,27,256]{3,0,2,1:T(8,128)(2,1)} %copy.27), channel_id=1, source_target_pairs={{0,16},{16,32},{32,48},{48,64},{64,80},{80,96},{96,112},{112,128},... | collective-permute-start | bytes 3981320 | tf_op jit(solution)/shard_map/ppermute | solution.py:19
  10.8 21.5 %collective-permute-start.1 = (bf16[16,6,27,256]{3,0,2,1:T(8,128)(2,1)}, bf16[16,6,27,256]{3,0,2,1:T(8,128)(2,1)}, u32[]{:S(2)}, u32[]{:S(2)}) collective-permute-start(bf16[16,6,27,256]{3,0,2,1:T(8,128)(2,1)} %copy.28), channel_id=1, source_target_pairs={{16,0},{32,16},{48,32},{64,48},{80,64},{96,80},{112,96},{128,112},... | collective-permute-start | bytes 3981320 | tf_op jit(solution)/shard_map/ppermute | solution.py:21
  45.2 9.1 %copy-start.2 = (s32[6,64,256]{2,1,0:T(8,128)S(1)}, s32[6,64,256]{2,1,0:T(8,128)}, u32[]{:S(2)}) copy-start(s32[6,64,256]{2,1,0:T(8,128)} %param.11) | copy-start | bytes 1179652
  45.2 17.8 %collective-permute-start.2 = (bf16[16,6,118,27]{2,0,3,1:T(8,128)(2,1)}, bf16[16,6,118,27]{2,0,3,1:T(8,128)(2,1)}, u32[]{:S(2)}, u32[]{:S(2)}) collective-permute-start(bf16[16,6,118,27]{2,0,3,1:T(8,128)(2,1)} %get-tuple-element.440), channel_id=1, source_target_pairs={{0,1},{1,2},{2,3},{3,4},{4,5},{5,6},{6,7},{7,8},{8,9},{9,10},{10,1... | collective-permute-start | bytes 1835144 | tf_op jit(solution)/shard_map/ppermute | solution.py:19
  48.4 19.5 %collective-permute-start.3 = (bf16[16,6,118,27]{2,0,3,1:T(8,128)(2,1)}, bf16[16,6,118,27]{2,0,3,1:T(8,128)(2,1)}, u32[]{:S(2)}, u32[]{:S(2)}) collective-permute-start(bf16[16,6,118,27]{2,0,3,1:T(8,128)(2,1)} %get-tuple-element.441), channel_id=1, source_target_pairs={{1,0},{2,1},{3,2},{4,3},{5,4},{6,5},{7,6},{8,7},{9,8},{10,9},{11,1... | collective-permute-start | bytes 1835144 | tf_op jit(solution)/shard_map/ppermute | solution.py:21
  92.4 10.6 %copy-start = (s32[6,64,256]{2,1,0:T(8,128)S(1)}, s32[6,64,256]{2,1,0:T(8,128)}, u32[]{:S(2)}) copy-start(s32[6,64,256]{2,1,0:T(8,128)} %param.10) | copy-start | bytes 1179652
  92.4 10.6 %copy-start.3 = (s32[12,3]{0,1:T(4,128)S(1)}, s32[12,3]{0,1:T(4,128)}, u32[]{:S(2)}) copy-start(s32[12,3]{0,1:T(4,128)} %param.9) | copy-start | bytes 436
  455.1 32.9 %collective-permute-start.4 = (f32[12,6,27,256]{3,2,1,0:T(8,128)}, f32[12,6,27,256]{3,2,1,0:T(8,128)}, u32[]{:S(2)}, u32[]{:S(2)}) collective-permute-start(f32[12,6,27,256]{3,2,1,0:T(8,128)} %get-tuple-element.442), channel_id=1, source_target_pairs={{0,16},{16,32},{32,48},{48,64},{64,80},{80,96},{96,112},{112,128},... | collective-permute-start | bytes 5971976 | tf_op jit(solution)/shard_map/ppermute | solution.py:19
  461.9 32.8 %collective-permute-start.5 = (f32[12,6,27,256]{3,2,1,0:T(8,128)S(1)}, f32[12,6,27,256]{3,2,1,0:T(8,128)}, u32[]{:S(2)}, u32[]{:S(2)}) collective-permute-start(f32[12,6,27,256]{3,2,1,0:T(8,128)S(1)} %get-tuple-element.443), channel_id=1, source_target_pairs={{16,0},{32,16},{48,32},{64,48},{80,64},{96,80},{112,96},{128,112},... | collective-permute-start | bytes 5971976 | tf_op jit(solution)/shard_map/ppermute | solution.py:21
  506.9 29.9 %collective-permute-start.6 = (f32[12,6,118,27]{2,3,1,0:T(8,128)}, f32[12,6,118,27]{2,3,1,0:T(8,128)S(1)}, u32[]{:S(2)}, u32[]{:S(2)}) collective-permute-start(f32[12,6,118,27]{2,3,1,0:T(8,128)} %get-tuple-element.438), channel_id=1, source_target_pairs={{0,1},{1,2},{2,3},{3,4},{4,5},{5,6},{6,7},{7,8},{8,9},{9,10},{10,1... | collective-permute-start | bytes 2752712 | tf_op jit(solution)/shard_map/ppermute | solution.py:19
  508.8 31.8 %collective-permute-start.7 = (f32[12,6,118,27]{2,3,1,0:T(8,128)S(1)}, f32[12,6,118,27]{2,3,1,0:T(8,128)S(1)}, u32[]{:S(2)}, u32[]{:S(2)}) collective-permute-start(f32[12,6,118,27]{2,3,1,0:T(8,128)S(1)} %get-tuple-element.439), channel_id=1, source_target_pairs={{1,0},{2,1},{3,2},{4,3},{5,4},{6,5},{7,6},{8,7},{9,8},{10,9},{11,1... | collective-permute-start | bytes 2752712 | tf_op jit(solution)/shard_map/ppermute | solution.py:21
where the time goes:
time: 804 us; the launch traced here: 800 us
  other arithmetic  434 us (54%)
  local copies, waits for them, and re-layouts  144 us (18%)
  loops' own time  134 us (17%)
  waiting for transfers between devices  62.4 us (8%)
  starting transfers between devices  25.8 us (3%)
    add x12, other arithmetic, forward_step(): return (own_acc + slope[None] * partner, slope)  127 us
    add x12, other arithmetic, return_step(): return own_acc + slope * source  124 us
    reduce_sum x12, other arithmetic, slope_of(): logits = jnp.sum(own_float * partner, axis=0)  90.6 us
    another operation x1, loops' own time, on_device(): return lax.fori_loop(0, K, return_step, own_grad)  68.4 us
    another operation x1, loops' own time, on_device(): lax.scan(forward_step, own_grad, jnp.arange(K, dtype=jnp.int32))  65.4 us
    ppermute x4, waiting for transfers between devices, with_halo(): lax.ppermute(tail, axis, [(i, (i + 1) % count) for i in range(ends)])  53.6 us
    unnamed x13, local copies, waits for them, and re-layouts  35.4 us
    concatenate x2, other arithmetic, with_halo(): jnp.concatenate([lax.ppermute(tail, axis, [(i, (i + 1) % count) for i in...  28.3 us
  transfers between devices with their start and end apart: 8, of which 6 were waited for; matrix products, arithmetic and copies ran while one was open for 4% of the time, Pallas kernels for 0%

commit v1 on v0

v1 whole, which is shorter than its diff:
```python
import functools

import jax
import jax.numpy as jnp
from jax import lax
from jax.experimental import pallas as pl
from jax.experimental.pallas import tpu as pltpu
from jax.sharding import PartitionSpec as P

HALO = 32
LANES = 128
SLOTS = LANES // HALO
LOW = 64
VMEM_BYTES = 56 << 20


def roll_to(value, source, dest):
    return value if source == dest else pltpu.roll(value, (dest - source) % LANES, 1)


def pack_kernel(e_ref, t_ref, m_ref, own_ref, first_ref, last_ref):
    channels, slices, rows, _ = e_ref.shape
    planes = channels + 2
    lane = lax.broadcasted_iota(jnp.int32, (rows, LANES), 1)
    for z in range(slices):
        for x in range(2):
            cols = slice(x * LANES, (x + 1) * LANES)
            for c in range(channels):
                own_ref[x, z, c] = e_ref[c, z, :, cols]
            code = t_ref[z, :, cols] | jnp.left_shift(m_ref[z, :, cols], 12)
            own_ref[x, z, channels] = (code & (LOW - 1)).astype(jnp.float32).astype(jnp.bfloat16)
            own_ref[x, z, channels + 1] = jnp.right_shift(code, 6).astype(jnp.float32).astype(jnp.bfloat16)
    for group in range(slices * planes // SLOTS):
        for x, out in ((0, first_ref), (1, last_ref)):
            packed = None
            for slot in range(SLOTS):
                z, c = divmod(group * SLOTS + slot, planes)
                moved = roll_to(own_ref[x, z, c], x * (LANES - HALO), slot * HALO)
                packed = moved if packed is None else jnp.where(lane >= slot * HALO, moved, packed)
            out[group] = packed


def pack(embedding, targets, mask):
    channels, slices, rows, cols = embedding.shape
    planes = channels + 2
    strip = jax.ShapeDtypeStruct((slices * planes // SLOTS, rows, LANES), jnp.bfloat16)
    return pl.pallas_call(
        pack_kernel,
        out_shape=(jax.ShapeDtypeStruct((2, slices, planes, rows, LANES), jnp.bfloat16), strip, strip),
        compiler_params=pltpu.CompilerParams(vmem_limit_bytes=VMEM_BYTES),
        name="pack",
    )(embedding, targets, mask)


def affinity_kernel(off_ref, own_ref, above_ref, below_ref, right_ref, left_ref, ra_ref, la_ref, rb_ref, lb_ref,
                    g_ref, f_ref, t_ref, m_ref, w_ref, *, per):
    _, nz, planes, own_rows, _ = own_ref.shape
    nc = planes - 2
    tiles = own_rows // 8
    lane = lax.broadcasted_iota(jnp.int32, (8, 128), 1)
    spans = (
        (0, HALO, above_ref, ra_ref, la_ref),
        (HALO, own_rows, own_ref, right_ref, left_ref),
        (HALO + own_rows, HALO, below_ref, rb_ref, lb_ref),
    )

    def decode(blk, z, at, low, high):
        code = (low.astype(jnp.float32) + LOW * high.astype(jnp.float32)).astype(jnp.int32)
        t_ref[blk, z, at, :] = code
        m_ref[blk, z, at, :] = jnp.right_shift(code, 12).astype(jnp.float32)

    for start, size, body_ref, r_ref, l_ref in spans:
        at = slice(start, start + size)
        wide = lax.broadcasted_iota(jnp.int32, (size, LANES), 1)

        def cast(z, _):
            for x in range(2):
                f_ref[1 + x, z, :, at, :] = body_ref[x, z, :nc].astype(jnp.float32)
                decode(1 + x, z, at, body_ref[x, z, nc], body_ref[x, z, nc + 1])
            return 0
        lax.fori_loop(0, nz, cast, 0)
        for z in range(nz):
            held = []
            for c in range(planes):
                group, slot = divmod(z * planes + c, SLOTS)
                from_right = roll_to(r_ref[group], slot * HALO, 0)
                from_left = roll_to(l_ref[group], slot * HALO, LANES - HALO)
                halo = jnp.where(wide < LANES // 2, from_right, from_left)
                if c < nc:
                    f_ref[0, z, c, at, :] = halo.astype(jnp.float32)
                else:
                    held.append(halo)
            decode(0, z, at, *held)

    rows = lax.broadcasted_iota(jnp.int32, (256, 256), 0)
    cols = lax.broadcasted_iota(jnp.int32, (256, 256), 1)

    def zero(i, _):
        g_ref[i] = jnp.zeros(g_ref.shape[1:], jnp.float32)
        return 0
    lax.fori_loop(0, nc, zero, 0)

    def pair(k, _):
        oz, oy, ox = off_ref[k, 0], off_ref[k, 1], off_ref[k, 2]
        bit = jnp.left_shift(1, k)
        lo = jnp.maximum(0, -oz)
        hi = jnp.minimum(nz, nz - oz)

        def shifted(slot, dx):
            w_ref[slot] = jnp.where(rows == ((cols + dx) & 255), 1.0, 0.0).astype(jnp.bfloat16)
            in0 = lane < dx
            in1 = lane >= 128 + dx
            def merge(h, a, b):
                return jnp.concatenate([jnp.where(in0, h, a), jnp.where(in1, h, b)], axis=1)
            return merge
        merge_f = shifted(0, ox)
        merge_b = shifted(1, -ox)

        def label(z, r0, blk):
            m = m_ref[blk, z, pl.ds(r0, 8), :]
            t = t_ref[blk, z, pl.ds(r0, 8), :]
            return jnp.where((t & bit) != 0, -m, m)

        def tile(t, own, src, dy, merge, slot, back):
            r0 = 32 + dy + t * 8
            parts = [merge(*(f_ref[blk, src, c, pl.ds(r0, 8), :] for blk in range(3))) for c in range(nc)]
            if back:
                lab = merge(*(label(src, r0, blk) for blk in range(3)))
                parts += [lab, lab]
            lhs = jnp.concatenate(parts, axis=0).astype(jnp.bfloat16)
            p = jnp.dot(lhs, w_ref[slot], preferred_element_type=jnp.float32)
            o0 = 32 + t * 8
            for x in range(2):
                xs = slice(x * 128, x * 128 + 128)
                q = [p[c * 8:c * 8 + 8, xs] for c in range(nc)]
                prods = [q[c] * f_ref[1 + x, own, c, o0:o0 + 8, :] for c in range(nc)]
                while len(prods) > 1:
                    prods = [u + v for u, v in zip(prods[::2], prods[1::2])]
                if back:
                    lab = p[nc * 8:nc * 8 + 8, xs]
                    keep = jnp.abs(lab)
                else:
                    lab = label(own, o0, 1 + x)
                    keep = m_ref[1 + x, own, o0:o0 + 8, :]
                s = keep * jnp.tanh(prods[0] * 0.5) + lab
                for c in range(nc):
                    g_ref[c, own, t * 8:t * 8 + 8, xs] += s * q[c]

        def plane(z, _):
            for t in range(0, tiles, per):
                for i in range(t, t + per):
                    tile(i, z, z + oz, oy, merge_f, 0, False)
                for i in range(t, t + per):
                    tile(i, z + oz, z, -oy, merge_b, 1, True)
            return 0
        lax.fori_loop(lo, hi, plane, 0)
        return 0
    lax.fori_loop(0, off_ref.shape[0], pair, 0)

    def half(i, _):
        g_ref[i] = g_ref[i] * 0.5
        return 0
    lax.fori_loop(0, nc, half, 0)


def affinity(off, own, *halos):
    _, nz, planes, rows, _ = own.shape
    nc = planes - 2
    V = pl.BlockSpec(memory_space=pltpu.VMEM)
    tall = rows + 2 * HALO
    return pl.pallas_call(
        functools.partial(affinity_kernel, per=8),
        out_shape=jax.ShapeDtypeStruct((nc, nz, rows, 2 * LANES), jnp.float32),
        in_specs=[pl.BlockSpec(memory_space=pltpu.SMEM)] + [V] * (1 + len(halos)),
        out_specs=V,
        scratch_shapes=[
            pltpu.VMEM((3, nz, nc, tall, LANES), jnp.float32),
            pltpu.VMEM((3, nz, tall, LANES), jnp.int32),
            pltpu.VMEM((3, nz, tall, LANES), jnp.float32),
            pltpu.VMEM((2, 256, 256), jnp.bfloat16),
        ],
        compiler_params=pltpu.CompilerParams(vmem_limit_bytes=VMEM_BYTES),
        name="affinity",
    )(off, own, *halos)


def send(value, axis, step):
    count = lax.axis_size(axis)
    return lax.ppermute(value, axis, [(i, i + step) for i in range(count) if 0 <= i + step < count])


def on_device(embedding, offsets, targets, mask):
    rows = embedding.shape[2]
    own, first, last = pack(embedding, targets, mask)
    from_above = send(own[..., rows - HALO:, :], "gy", 1)
    from_below = send(own[..., :HALO, :], "gy", -1)
    right = send(first, "gx", -1)
    left = send(last, "gx", 1)
    corners_above = [send(v[:, rows - HALO:], "gy", 1) for v in (right, left)]
    corners_below = [send(v[:, :HALO], "gy", -1) for v in (right, left)]
    return affinity(offsets, own, from_above, from_below, right, left, *corners_above, *corners_below)


def solution(mesh):
    return jax.shard_map(
        on_device,
        mesh=mesh,
        in_specs=(P(None, None, "gy", "gx"), P(), P(None, "gy", "gx"), P(None, "gy", "gx")),
        out_specs=P(None, None, "gy", "gx"),
        check_vma=False,
    )
```

time: 804 us -> 115 us (0.14)
  the two profiles are of different devices: /device:TPU:71 before, /device:TPU:150 now
where the time goes in v1:
time: 115 us; the launch traced here: 114 us
  Pallas kernels  69.2 us (60%)
  starting transfers between devices  23 us (20%)
  waiting for transfers between devices  15 us (13%)
  local copies, waits for them, and re-layouts  7.15 us (6%)
    pallas_call x1, Pallas kernels, affinity(): pl.pallas_call(functools.partial(affinity_kernel, per=8), out_shape=jax.S...  64.2 us
    ppermute x8, starting transfers between devices, send(): lax.ppermute(value, axis, [(i, i + step) for i in range(count) if 0 <= i...  23 us
    ppermute x8, waiting for transfers between devices, send(): lax.ppermute(value, axis, [(i, i + step) for i in range(count) if 0 <= i...  15 us
    pallas_call x1, Pallas kernels, pack(): pl.pallas_call(pack_kernel, out_shape=(jax.ShapeDtypeStruct((2, slices, p...  5 us
    slice x1, local copies, waits for them, and re-layouts, on_device(): from_below = send(own[..., :HALO, :], 'gy', -1)  4.11 us
  transfers between devices with their start and end apart: 8, of which 3 were waited for; matrix products, arithmetic and copies ran while one was open for 2% of the time, Pallas kernels for 0%

profile of v1, /device:TPU:150, one launch (start us, length us, event | category | flops | bytes accessed | tf_op | source)
XLA Modules:
  0.0 114.5 jit_solution(5567847115998690181)
XLA Ops:
  0.0 5.0 %pack.1 = (bf16[2,6,18,64,128]{4,3,2,1,0:T(8,128)(2,1)}, bf16[27,64,128]{2,1,0:T(8,128)(2,1)}, bf16[27,64,128]{2,1,0:T(8,128)(2,1)}) custom-call(bf16[16,6,64,256]{3,2,1,0:T(8,128)(2,1)} %e_ref.1, s32[6,64,256]{2,1,0:T(8,128)} %t_ref.1, s32[6,64,256]{2,1,0:T(8,128)} %m_ref.1), custom_call_target="tpu_custom_call" | custom-call | tf_op jit(solution)/shard_map/pack/pallas_call | solution.py:47
  5.0 0.0 copy-start.8
  5.0 0.0 copy-start.7
  5.0 4.1 %fusion = (bf16[2,6,18,32,128]{4,3,2,1,0:T(8,128)(2,1)}, bf16[2,6,18,32,128]{4,3,2,1,0:T(8,128)(2,1)S(1)}) fusion(bf16[2,6,18,64,128]{4,3,2,1,0:T(8,128)(2,1)} %get-tuple-element.8.own_ref), kind=kLoop, calls=%fused_computation | loop fusion | bytes 7077888 | tf_op jit(solution)/shard_map/slice | solution.py:196
  9.1 0.0 copy-start.6
  9.1 2.0 %collective-permute-start.1 = (bf16[2,6,18,32,128]{4,3,2,1,0:T(8,128)(2,1)}, bf16[2,6,18,32,128]{4,3,2,1,0:T(8,128)(2,1)}, u32[]{:S(2)}, u32[]{:S(2)}) collective-permute-start(bf16[2,6,18,32,128]{4,3,2,1,0:T(8,128)(2,1)} %get-tuple-element.11), channel_id=1, source_target_pairs={{16,0},{32,16},{48,32},{64,48},{80,64},{96,80},{112,96},{128,112},... | collective-permute-start | bytes 5308424 | tf_op jit(solution)/shard_map/ppermute | solution.py:189
  11.2 2.4 %collective-permute-start = (bf16[2,6,18,32,128]{4,3,2,1,0:T(8,128)(2,1)S(1)}, bf16[2,6,18,32,128]{4,3,2,1,0:T(8,128)(2,1)}, u32[]{:S(2)}, u32[]{:S(2)}) collective-permute-start(bf16[2,6,18,32,128]{4,3,2,1,0:T(8,128)(2,1)S(1)} %get-tuple-element.12), channel_id=1, source_target_pairs={{0,16},{16,32},{32,48},{48,64},{64,80},{80,96},{96,112},{112,128},... | collective-permute-start | bytes 5308424 | tf_op jit(solution)/shard_map/ppermute | solution.py:189
  13.6 0.0 copy-done.8
  13.6 2.7 %collective-permute-start.2 = (bf16[27,64,128]{2,1,0:T(8,128)(2,1)S(1)}, bf16[27,64,128]{2,1,0:T(8,128)(2,1)S(1)}, u32[]{:S(2)}, u32[]{:S(2)}) collective-permute-start(bf16[27,64,128]{2,1,0:T(8,128)(2,1)S(1)} %copy-done.8), channel_id=1, source_target_pairs={{1,0},{2,1},{3,2},{4,3},{5,4},{6,5},{7,6},{8,7},{9,8},{10,9},{11,1... | collective-permute-start | bytes 1327112 | tf_op jit(solution)/shard_map/ppermute | solution.py:189
  16.3 0.0 copy-done.7
  16.3 5.2 %collective-permute-start.3 = (bf16[27,64,128]{2,1,0:T(8,128)(2,1)S(1)}, bf16[27,64,128]{2,1,0:T(8,128)(2,1)S(1)}, u32[]{:S(2)}, u32[]{:S(2)}) collective-permute-start(bf16[27,64,128]{2,1,0:T(8,128)(2,1)S(1)} %copy-done.7), channel_id=1, source_target_pairs={{0,1},{1,2},{2,3},{3,4},{4,5},{5,6},{6,7},{7,8},{8,9},{9,10},{10,1... | collective-permute-start | bytes 1327112 | tf_op jit(solution)/shard_map/ppermute | solution.py:189
  21.6 9.0 %collective-permute-done.2.right_ref = bf16[27,64,128]{2,1,0:T(8,128)(2,1)S(1)} collective-permute-done((bf16[27,64,128]{2,1,0:T(8,128)(2,1)S(1)}, bf16[27,64,128]{2,1,0:T(8,128)(2,1)S(1)}, u32[]{:S(2)}, u32[]{:S(2)}) %collective-permute-start.2) | collective-permute-done | bytes 442400 | tf_op jit(solution)/shard_map/ppermute | solution.py:189
  30.5 0.0 copy-start
  30.5 0.8 fusion.2
  31.3 1.9 %collective-permute-start.6 = (bf16[27,32,128]{2,1,0:T(8,128)(2,1)S(1)}, bf16[27,32,128]{2,1,0:T(8,128)(2,1)S(1)}, u32[]{:S(2)}, u32[]{:S(2)}) collective-permute-start(bf16[27,32,128]{2,1,0:T(8,128)(2,1)S(1)} %get-tuple-element.15), channel_id=1, source_target_pairs={{16,0},{32,16},{48,32},{64,48},{80,64},{96,80},{112,96},{128,112},... | collective-permute-start | bytes 663560 | tf_op jit(solution)/shard_map/ppermute | solution.py:189
  33.2 2.4 %collective-permute-start.4 = (bf16[27,32,128]{2,1,0:T(8,128)(2,1)}, bf16[27,32,128]{2,1,0:T(8,128)(2,1)S(1)}, u32[]{:S(2)}, u32[]{:S(2)}) collective-permute-start(bf16[27,32,128]{2,1,0:T(8,128)(2,1)} %get-tuple-element.16), channel_id=1, source_target_pairs={{0,16},{16,32},{32,48},{48,64},{64,80},{80,96},{96,112},{112,128},... | collective-permute-start | bytes 663560 | tf_op jit(solution)/shard_map/ppermute | solution.py:189
  35.6 0.0 collective-permute-done.3.left_ref
  35.6 0.0 copy-start.1
  35.7 0.9 fusion.1
  36.6 4.4 %collective-permute-start.7 = (bf16[27,32,128]{2,1,0:T(8,128)(2,1)}, bf16[27,32,128]{2,1,0:T(8,128)(2,1)S(1)}, u32[]{:S(2)}, u32[]{:S(2)}) collective-permute-start(bf16[27,32,128]{2,1,0:T(8,128)(2,1)} %get-tuple-element.13), channel_id=1, source_target_pairs={{16,0},{32,16},{48,32},{64,48},{80,64},{96,80},{112,96},{128,112},... | collective-permute-start | bytes 663560 | tf_op jit(solution)/shard_map/ppermute | solution.py:189
  40.9 0.0 collective-permute-done.6.rb_ref
  40.9 0.0 copy-start.2
  41.0 1.9 %collective-permute-start.5 = (bf16[27,32,128]{2,1,0:T(8,128)(2,1)}, bf16[27,32,128]{2,1,0:T(8,128)(2,1)S(1)}, u32[]{:S(2)}, u32[]{:S(2)}) collective-permute-start(bf16[27,32,128]{2,1,0:T(8,128)(2,1)} %get-tuple-element.14), channel_id=1, source_target_pairs={{0,16},{16,32},{32,48},{48,64},{64,80},{80,96},{96,112},{112,128},... | collective-permute-start | bytes 663560 | tf_op jit(solution)/shard_map/ppermute | solution.py:189
  42.9 0.0 copy-done.6
  42.9 0.7 copy.5.off_ref
  43.6 0.0 collective-permute-done.4.ra_ref
  43.6 0.0 copy-start.3
  43.6 1.1 collective-permute-done.7.lb_ref
  44.7 0.0 copy-start.4
  44.7 4.9 %collective-permute-done.5.la_ref = bf16[27,32,128]{2,1,0:T(8,128)(2,1)S(1)} collective-permute-done((bf16[27,32,128]{2,1,0:T(8,128)(2,1)}, bf16[27,32,128]{2,1,0:T(8,128)(2,1)S(1)}, u32[]{:S(2)}, u32[]{:S(2)}) %collective-permute-start.5) | collective-permute-done | bytes 221216 | tf_op jit(solution)/shard_map/ppermute | solution.py:189
  49.6 0.0 copy-start.5
  49.6 0.0 collective-permute-done.1.below_ref
  49.6 0.0 collective-permute-done.above_ref
  49.6 0.0 copy-done
  49.6 0.0 copy-done.1
  49.7 0.0 copy-done.2
  49.7 0.0 copy-done.3
  49.7 0.0 copy-done.4
  49.7 0.6 copy-done.5
  50.3 64.2 %affinity.1 = f32[16,6,64,256]{3,2,1,0:T(8,128)} custom-call(s32[12,3]{1,0:T(8,128)} %copy.5.off_ref, bf16[2,6,18,64,128]{4,3,2,1,0:T(8,128)(2,1)} %get-tuple-element.8.own_ref, bf16[2,6,18,32,128]{4,3,2,1,0:T(8,128)(2,1)} %collective-permute-done.above_ref, bf16[2,6,18,32,128]{4,3,2,1,0:T(8,128)(2,1)} %collective-permute-done.1.below_ref, ...), custom_call_target="tpu_custom_call" | custom-call | tf_op jit(solution)/shard_map/affinity/pallas_call | solution.py:171
Async XLA Ops:
  5.0 8.6 %copy-start.8 = (bf16[27,64,128]{2,1,0:T(8,128)(2,1)S(1)}, bf16[27,64,128]{2,1,0:T(8,128)(2,1)}, u32[]{:S(2)}) copy-start(bf16[27,64,128]{2,1,0:T(8,128)(2,1)} %get-tuple-element.9) | copy-start | bytes 1327108
  5.0 11.3 %copy-start.7 = (bf16[27,64,128]{2,1,0:T(8,128)(2,1)S(1)}, bf16[27,64,128]{2,1,0:T(8,128)(2,1)}, u32[]{:S(2)}) copy-start(bf16[27,64,128]{2,1,0:T(8,128)(2,1)} %get-tuple-element.10) | copy-start | bytes 1327108
  9.1 33.8 %copy-start.6 = (s32[12,3]{0,1:T(4,128)S(1)}, s32[12,3]{0,1:T(4,128)}, u32[]{:S(2)}) copy-start(s32[12,3]{0,1:T(4,128)} %param.5) | copy-start | bytes 436
  9.1 40.5 %collective-permute-start.1 = (bf16[2,6,18,32,128]{4,3,2,1,0:T(8,128)(2,1)}, bf16[2,6,18,32,128]{4,3,2,1,0:T(8,128)(2,1)}, u32[]{:S(2)}, u32[]{:S(2)}) collective-permute-start(bf16[2,6,18,32,128]{4,3,2,1,0:T(8,128)(2,1)} %get-tuple-element.11), channel_id=1, source_target_pairs={{16,0},{32,16},{48,32},{64,48},{80,64},{96,80},{112,96},{128,112},... | collective-permute-start | bytes 5308424 | tf_op jit(solution)/shard_map/ppermute | solution.py:189
  11.2 38.5 %collective-permute-start = (bf16[2,6,18,32,128]{4,3,2,1,0:T(8,128)(2,1)S(1)}, bf16[2,6,18,32,128]{4,3,2,1,0:T(8,128)(2,1)}, u32[]{:S(2)}, u32[]{:S(2)}) collective-permute-start(bf16[2,6,18,32,128]{4,3,2,1,0:T(8,128)(2,1)S(1)} %get-tuple-element.12), channel_id=1, source_target_pairs={{0,16},{16,32},{32,48},{48,64},{64,80},{80,96},{96,112},{112,128},... | collective-permute-start | bytes 5308424 | tf_op jit(solution)/shard_map/ppermute | solution.py:189
  13.6 16.9 %collective-permute-start.2 = (bf16[27,64,128]{2,1,0:T(8,128)(2,1)S(1)}, bf16[27,64,128]{2,1,0:T(8,128)(2,1)S(1)}, u32[]{:S(2)}, u32[]{:S(2)}) collective-permute-start(bf16[27,64,128]{2,1,0:T(8,128)(2,1)S(1)} %copy-done.8), channel_id=1, source_target_pairs={{1,0},{2,1},{3,2},{4,3},{5,4},{6,5},{7,6},{8,7},{9,8},{10,9},{11,1... | collective-permute-start | bytes 1327112 | tf_op jit(solution)/shard_map/ppermute | solution.py:189
  16.3 19.3 %collective-permute-start.3 = (bf16[27,64,128]{2,1,0:T(8,128)(2,1)S(1)}, bf16[27,64,128]{2,1,0:T(8,128)(2,1)S(1)}, u32[]{:S(2)}, u32[]{:S(2)}) collective-permute-start(bf16[27,64,128]{2,1,0:T(8,128)(2,1)S(1)} %copy-done.7), channel_id=1, source_target_pairs={{0,1},{1,2},{2,3},{3,4},{4,5},{5,6},{6,7},{7,8},{8,9},{9,10},{10,1... | collective-permute-start | bytes 1327112 | tf_op jit(solution)/shard_map/ppermute | solution.py:189
  30.5 19.1 %copy-start = (bf16[27,64,128]{2,1,0:T(8,128)(2,1)}, bf16[27,64,128]{2,1,0:T(8,128)(2,1)S(1)}, u32[]{:S(2)}) copy-start(bf16[27,64,128]{2,1,0:T(8,128)(2,1)S(1)} %collective-permute-done.2.right_ref) | copy-start | bytes 1327108
  31.3 9.6 %collective-permute-start.6 = (bf16[27,32,128]{2,1,0:T(8,128)(2,1)S(1)}, bf16[27,32,128]{2,1,0:T(8,128)(2,1)S(1)}, u32[]{:S(2)}, u32[]{:S(2)}) collective-permute-start(bf16[27,32,128]{2,1,0:T(8,128)(2,1)S(1)} %get-tuple-element.15), channel_id=1, source_target_pairs={{16,0},{32,16},{48,32},{64,48},{80,64},{96,80},{112,96},{128,112},... | collective-permute-start | bytes 663560 | tf_op jit(solution)/shard_map/ppermute | solution.py:189
  33.2 10.4 %collective-permute-start.4 = (bf16[27,32,128]{2,1,0:T(8,128)(2,1)}, bf16[27,32,128]{2,1,0:T(8,128)(2,1)S(1)}, u32[]{:S(2)}, u32[]{:S(2)}) collective-permute-start(bf16[27,32,128]{2,1,0:T(8,128)(2,1)} %get-tuple-element.16), channel_id=1, source_target_pairs={{0,16},{16,32},{32,48},{48,64},{64,80},{80,96},{96,112},{112,128},... | collective-permute-start | bytes 663560 | tf_op jit(solution)/shard_map/ppermute | solution.py:189
  35.6 14.0 %copy-start.1 = (bf16[27,64,128]{2,1,0:T(8,128)(2,1)}, bf16[27,64,128]{2,1,0:T(8,128)(2,1)S(1)}, u32[]{:S(2)}) copy-start(bf16[27,64,128]{2,1,0:T(8,128)(2,1)S(1)} %collective-permute-done.3.left_ref) | copy-start | bytes 1327108
  36.6 8.1 %collective-permute-start.7 = (bf16[27,32,128]{2,1,0:T(8,128)(2,1)}, bf16[27,32,128]{2,1,0:T(8,128)(2,1)S(1)}, u32[]{:S(2)}, u32[]{:S(2)}) collective-permute-start(bf16[27,32,128]{2,1,0:T(8,128)(2,1)} %get-tuple-element.13), channel_id=1, source_target_pairs={{16,0},{32,16},{48,32},{64,48},{80,64},{96,80},{112,96},{128,112},... | collective-permute-start | bytes 663560 | tf_op jit(solution)/shard_map/ppermute | solution.py:189
  40.9 8.7 %copy-start.2 = (bf16[27,32,128]{2,1,0:T(8,128)(2,1)}, bf16[27,32,128]{2,1,0:T(8,128)(2,1)S(1)}, u32[]{:S(2)}) copy-start(bf16[27,32,128]{2,1,0:T(8,128)(2,1)S(1)} %collective-permute-done.6.rb_ref) | copy-start | bytes 663556
  41.0 8.7 %collective-permute-start.5 = (bf16[27,32,128]{2,1,0:T(8,128)(2,1)}, bf16[27,32,128]{2,1,0:T(8,128)(2,1)S(1)}, u32[]{:S(2)}, u32[]{:S(2)}) collective-permute-start(bf16[27,32,128]{2,1,0:T(8,128)(2,1)} %get-tuple-element.14), channel_id=1, source_target_pairs={{0,16},{16,32},{32,48},{48,64},{64,80},{80,96},{96,112},{112,128},... | collective-permute-start | bytes 663560 | tf_op jit(solution)/shard_map/ppermute | solution.py:189
  43.6 6.1 %copy-start.3 = (bf16[27,32,128]{2,1,0:T(8,128)(2,1)}, bf16[27,32,128]{2,1,0:T(8,128)(2,1)S(1)}, u32[]{:S(2)}) copy-start(bf16[27,32,128]{2,1,0:T(8,128)(2,1)S(1)} %collective-permute-done.4.ra_ref) | copy-start | bytes 663556
  44.7 5.0 %copy-start.4 = (bf16[27,32,128]{2,1,0:T(8,128)(2,1)}, bf16[27,32,128]{2,1,0:T(8,128)(2,1)S(1)}, u32[]{:S(2)}) copy-start(bf16[27,32,128]{2,1,0:T(8,128)(2,1)S(1)} %collective-permute-done.7.lb_ref) | copy-start | bytes 663556
  49.6 0.7 copy-start.5

commit v2 on v1

v2 whole, which is shorter than its diff:
```python
import functools

import jax
import jax.numpy as jnp
from jax import lax
from jax.experimental import pallas as pl
from jax.experimental.pallas import tpu as pltpu
from jax.sharding import PartitionSpec as P

MESH = pl.DeviceIdType.MESH
HALO = 32
LANES = 128
SLOTS = LANES // HALO
LOW = 64
VMEM_BYTES = 56 << 20


def roll_to(value, source, dest):
    return value if source == dest else pltpu.roll(value, (dest - source) % LANES, 1)


def exchange_kernel(e_ref, t_ref, m_ref, body_ref, side_ref, strip_ref, copied, sent, received):
    channels, slices, rows, _ = e_ref.shape
    planes = channels + 2
    groups = strip_ref.shape[1]
    me_y, me_x = lax.axis_index("gy"), lax.axis_index("gx")
    count_y, count_x = lax.axis_size("gy"), lax.axis_size("gx")
    below, above = (lax.rem(me_y + 1, count_y), me_x), (lax.rem(me_y + count_y - 1, count_y), me_x)
    right, left = (me_y, lax.rem(me_x + 1, count_x)), (me_y, lax.rem(me_x + count_x - 1, count_x))
    mine, tail, head = pl.ds(HALO, rows), pl.ds(rows, HALO), pl.ds(HALO, HALO)
    top, bottom = pl.ds(0, HALO), pl.ds(HALO + rows, HALO)

    own = [
        pltpu.make_async_copy(
            e_ref.at[:, :, :, pl.ds(x * LANES, LANES)], body_ref.at[x, pl.ds(0, channels), :, mine], copied.at[x]
        )
        for x in range(2)
    ]
    for copy in own:
        copy.start()

    barrier = pltpu.get_barrier_semaphore()
    for neighbour in (below, above, right, left):
        pl.semaphore_signal(barrier, inc=1, device_id=neighbour, device_id_type=MESH)
    pl.semaphore_wait(barrier, 4)

    def remote(index, source, target, device):
        copy = pltpu.make_async_remote_copy(
            src_ref=source, dst_ref=target, send_sem=sent.at[index], recv_sem=received.at[index],
            device_id=device, device_id_type=MESH,
        )
        copy.start()
        return copy

    inner = pl.ds(0, channels)
    flights = []
    for x in range(2):
        cols = pl.ds(x * LANES, LANES)
        flights.append(remote(x, e_ref.at[:, :, pl.ds(rows - HALO, HALO), cols], body_ref.at[x, inner, :, top], below))
        flights.append(remote(2 + x, e_ref.at[:, :, pl.ds(0, HALO), cols], body_ref.at[x, inner, :, bottom], above))

    for z in range(slices):
        for x in range(2):
            cols = slice(x * LANES, (x + 1) * LANES)
            code = t_ref[z, :, cols] | jnp.left_shift(m_ref[z, :, cols], 12)
            body_ref[x, channels, z, HALO:HALO + rows] = (code & (LOW - 1)).astype(jnp.float32).astype(jnp.bfloat16)
            body_ref[x, channels + 1, z, HALO:HALO + rows] = jnp.right_shift(code, 6).astype(jnp.float32).astype(jnp.bfloat16)
    codes = pl.ds(channels, 2)
    flights.append(remote(4, body_ref.at[:, codes, :, tail], body_ref.at[:, codes, :, top], below))
    flights.append(remote(5, body_ref.at[:, codes, :, head], body_ref.at[:, codes, :, bottom], above))

    for copy in own:
        copy.wait()
    lane = lax.broadcasted_iota(jnp.int32, (rows, LANES), 1)
    across = []
    for x, device in ((1, right), (0, left)):
        for group in range(groups):
            packed = None
            for slot in range(SLOTS):
                c, z = divmod(group * SLOTS + slot, slices)
                moved = roll_to(body_ref[x, c, z, HALO:HALO + rows], x * (LANES - HALO), slot * HALO)
                packed = moved if packed is None else jnp.where(lane >= slot * HALO, moved, packed)
            strip_ref[x, group] = packed
        across.append(remote(6 + x, strip_ref.at[x], side_ref.at[x, :, mine], device))
    for copy in across:
        copy.wait()

    corners = [
        remote(8, side_ref.at[:, :, tail], side_ref.at[:, :, top], below),
        remote(9, side_ref.at[:, :, head], side_ref.at[:, :, bottom], above),
    ]
    for copy in flights + corners:
        copy.wait()

    @pl.when(me_y == 0)
    def _():
        body_ref[:, :, :, 0:HALO] = jnp.zeros((2, planes, slices, HALO, LANES), jnp.bfloat16)
        side_ref[:, :, 0:HALO] = jnp.zeros((2, groups, HALO, LANES), jnp.bfloat16)

    @pl.when(me_y == count_y - 1)
    def _():
        body_ref[:, :, :, HALO + rows:] = jnp.zeros((2, planes, slices, HALO, LANES), jnp.bfloat16)
        side_ref[:, :, HALO + rows:] = jnp.zeros((2, groups, HALO, LANES), jnp.bfloat16)

    @pl.when(me_x == 0)
    def _():
        side_ref[1] = jnp.zeros(side_ref.shape[1:], jnp.bfloat16)

    @pl.when(me_x == count_x - 1)
    def _():
        side_ref[0] = jnp.zeros(side_ref.shape[1:], jnp.bfloat16)


def exchange(embedding, targets, mask):
    channels, slices, rows, cols = embedding.shape
    planes = channels + 2
    groups = slices * planes // SLOTS
    tall = rows + 2 * HALO
    V = pl.BlockSpec(memory_space=pltpu.VMEM)
    return pl.pallas_call(
        exchange_kernel,
        out_shape=(
            jax.ShapeDtypeStruct((2, planes, slices, tall, LANES), jnp.bfloat16),
            jax.ShapeDtypeStruct((2, groups, tall, LANES), jnp.bfloat16),
        ),
        in_specs=[pl.BlockSpec(memory_space=pl.ANY), V, V],
        out_specs=(V, V),
        scratch_shapes=[
            pltpu.VMEM((2, groups, rows, LANES), jnp.bfloat16),
            pltpu.SemaphoreType.DMA((2,)),
            pltpu.SemaphoreType.DMA((10,)),
            pltpu.SemaphoreType.DMA((10,)),
        ],
        compiler_params=pltpu.CompilerParams(
            collective_id=0, has_side_effects=True, vmem_limit_bytes=VMEM_BYTES
        ),
        name="exchange",
    )(embedding, targets, mask)


def affinity_kernel(off_ref, body_ref, side_ref, g_ref, f_ref, t_ref, m_ref, w_ref, *, per):
    _, planes, nz, tall, _ = body_ref.shape
    nc = planes - 2
    tiles = (tall - 2 * HALO) // 8
    lane = lax.broadcasted_iota(jnp.int32, (8, 128), 1)
    wide = lax.broadcasted_iota(jnp.int32, (tall, LANES), 1)

    def halo(c, z):
        group, slot = divmod(c * nz + z, SLOTS)
        from_right = roll_to(side_ref[0, group], slot * HALO, 0)
        from_left = roll_to(side_ref[1, group], slot * HALO, LANES - HALO)
        return jnp.where(wide < LANES // 2, from_right, from_left)

    def decode(blk, z, low, high):
        code = (low.astype(jnp.float32) + LOW * high.astype(jnp.float32)).astype(jnp.int32)
        t_ref[blk, z] = code
        m_ref[blk, z] = jnp.right_shift(code, 12).astype(jnp.float32)

    def cast(c, _):
        for x in range(2):
            f_ref[1 + x, c] = body_ref[x, c].astype(jnp.float32)
        return 0
    lax.fori_loop(0, nc, cast, 0)
    for c in range(nc):
        for z in range(nz):
            f_ref[0, c, z] = halo(c, z).astype(jnp.float32)
    for z in range(nz):
        for x in range(2):
            decode(1 + x, z, body_ref[x, nc, z], body_ref[x, nc + 1, z])
        decode(0, z, halo(nc, z), halo(nc + 1, z))

    rows = lax.broadcasted_iota(jnp.int32, (256, 256), 0)
    cols = lax.broadcasted_iota(jnp.int32, (256, 256), 1)

    def zero(i, _):
        g_ref[i] = jnp.zeros(g_ref.shape[1:], jnp.float32)
        return 0
    lax.fori_loop(0, nc, zero, 0)

    def pair(k, _):
        oz, oy, ox = off_ref[k, 0], off_ref[k, 1], off_ref[k, 2]
        bit = jnp.left_shift(1, k)
        lo = jnp.maximum(0, -oz)
        hi = jnp.minimum(nz, nz - oz)

        def shifted(slot, dx):
            w_ref[slot] = jnp.where(rows == ((cols + dx) & 255), 1.0, 0.0).astype(jnp.bfloat16)
            in0 = lane < dx
            in1 = lane >= 128 + dx
            def merge(h, a, b):
                return jnp.concatenate([jnp.where(in0, h, a), jnp.where(in1, h, b)], axis=1)
            return merge
        merge_f = shifted(0, ox)
        merge_b = shifted(1, -ox)

        def label(z, r0, blk):
            m = m_ref[blk, z, pl.ds(r0, 8), :]
            t = t_ref[blk, z, pl.ds(r0, 8), :]
            return jnp.where((t & bit) != 0, -m, m)

        def tile(t, own, src, dy, merge, slot, back):
            r0 = 32 + dy + t * 8
            parts = [merge(*(f_ref[blk, c, src, pl.ds(r0, 8), :] for blk in range(3))) for c in range(nc)]
            if back:
                lab = merge(*(label(src, r0, blk) for blk in range(3)))
                parts += [lab, lab]
            lhs = jnp.concatenate(parts, axis=0).astype(jnp.bfloat16)
            p = jnp.dot(lhs, w_ref[slot], preferred_element_type=jnp.float32)
            o0 = 32 + t * 8
            for x in range(2):
                xs = slice(x * 128, x * 128 + 128)
                q = [p[c * 8:c * 8 + 8, xs] for c in range(nc)]
                prods = [q[c] * f_ref[1 + x, c, own, o0:o0 + 8, :] for c in range(nc)]
                while len(prods) > 1:
                    prods = [u + v for u, v in zip(prods[::2], prods[1::2])]
                if back:
                    lab = p[nc * 8:nc * 8 + 8, xs]
                    keep = jnp.abs(lab)
                else:
                    lab = label(own, o0, 1 + x)
                    keep = m_ref[1 + x, own, o0:o0 + 8, :]
                s = keep * jnp.tanh(prods[0] * 0.5) + lab
                for c in range(nc):
                    g_ref[c, own, t * 8:t * 8 + 8, xs] += s * q[c]

        def plane(z, _):
            for t in range(0, tiles, per):
                for i in range(t, t + per):
                    tile(i, z, z + oz, oy, merge_f, 0, False)
                for i in range(t, t + per):
                    tile(i, z + oz, z, -oy, merge_b, 1, True)
            return 0
        lax.fori_loop(lo, hi, plane, 0)
        return 0
    lax.fori_loop(0, off_ref.shape[0], pair, 0)

    def half(i, _):
        g_ref[i] = g_ref[i] * 0.5
        return 0
    lax.fori_loop(0, nc, half, 0)


def affinity(off, body, side):
    _, planes, nz, tall, _ = body.shape
    nc = planes - 2
    V = pl.BlockSpec(memory_space=pltpu.VMEM)
    return pl.pallas_call(
        functools.partial(affinity_kernel, per=8),
        out_shape=jax.ShapeDtypeStruct((nc, nz, tall - 2 * HALO, 2 * LANES), jnp.float32),
        in_specs=[pl.BlockSpec(memory_space=pltpu.SMEM), V, V],
        out_specs=V,
        scratch_shapes=[
            pltpu.VMEM((3, nc, nz, tall, LANES), jnp.float32),
            pltpu.VMEM((3, nz, tall, LANES), jnp.int32),
            pltpu.VMEM((3, nz, tall, LANES), jnp.float32),
            pltpu.VMEM((2, 256, 256), jnp.bfloat16),
        ],
        compiler_params=pltpu.CompilerParams(vmem_limit_bytes=VMEM_BYTES),
        name="affinity",
    )(off, body, side)


def on_device(embedding, offsets, targets, mask):
    return affinity(offsets, *exchange(embedding, targets, mask))


def solution(mesh):
    return jax.shard_map(
        on_device,
        mesh=mesh,
        in_specs=(P(None, None, "gy", "gx"), P(), P(None, "gy", "gx"), P(None, "gy", "gx")),
        out_specs=P(None, None, "gy", "gx"),
        check_vma=False,
    )
```

time: 115 us -> 98.5 us (0.86)
  the two profiles are of different devices: /device:TPU:150 before, /device:TPU:0 now
where the time goes in v2:
time: 98.5 us; the launch traced here: 98.4 us
  Pallas kernels  97 us (98%)
  local copies, waits for them, and re-layouts  1.36 us (1%)
    pallas_call x1, Pallas kernels, affinity(): pl.pallas_call(functools.partial(affinity_kernel, per=8), out_shape=jax.S...  58.2 us
    pallas_call x1, Pallas kernels, exchange(): pl.pallas_call(exchange_kernel, out_shape=(jax.ShapeDtypeStruct((2, plane...  38.8 us

profile of v2, /device:TPU:0, one launch (start us, length us, event | category | flops | bytes accessed | tf_op | source)
XLA Modules:
  0.0 98.4 jit_solution(16396771411871789844)
XLA Ops:
  0.0 1.4 %copy.5.off_ref = s32[12,3]{1,0:T(8,128)} copy(s32[12,3]{0,1:T(4,128)} %param.5) | data formatting | bytes 288 | tf_op args[1]
  1.4 38.8 %exchange.1 = (bf16[2,18,6,128,128]{4,3,2,1,0:T(8,128)(2,1)}, bf16[2,27,128,128]{3,2,1,0:T(8,128)(2,1)}) custom-call(bf16[16,6,64,256]{3,2,1,0:T(8,128)(2,1)} %e_ref.1, s32[6,64,256]{2,1,0:T(8,128)} %t_ref.1, s32[6,64,256]{2,1,0:T(8,128)} %m_ref.1), custom_call_target="tpu_custom_call" | custom-call | tf_op jit(solution)/shard_map/exchange/pallas_call | solution.py:120
  40.2 58.2 %affinity.1 = f32[16,6,64,256]{3,2,1,0:T(8,128)} custom-call(s32[12,3]{1,0:T(8,128)} %copy.5.off_ref, bf16[2,18,6,128,128]{4,3,2,1,0:T(8,128)(2,1)} %get-tuple-element.7.body_ref, bf16[2,27,128,128]{3,2,1,0:T(8,128)(2,1)} %get-tuple-element.8.side_ref), custom_call_target="tpu_custom_call" | custom-call | tf_op jit(solution)/shard_map/affinity/pallas_call | solution.py:247

commit v3 on v2

--- a/solution.py
+++ b/solution.py
@@ -1,5 +1,3 @@
-import functools
-
 import jax
 import jax.numpy as jnp
 from jax import lax
@@ -12,7 +10,8 @@
 LANES = 128
 SLOTS = LANES // HALO
 LOW = 64
-VMEM_BYTES = 56 << 20
+VMEM_BYTES = 58 << 20
+PAD = 8
 
 
 def roll_to(value, source, dest):
@@ -138,7 +137,7 @@
     )(embedding, targets, mask)
 
 
-def affinity_kernel(off_ref, body_ref, side_ref, g_ref, f_ref, t_ref, m_ref, w_ref, *, per):
+def affinity_kernel(off_ref, body_ref, side_ref, g_ref, f_ref, t_ref, m_ref, gf_ref, gb_ref):
     _, planes, nz, tall, _ = body_ref.shape
     nc = planes - 2
     tiles = (tall - 2 * HALO) // 8
@@ -158,59 +157,69 @@
 
     def cast(c, _):
         for x in range(2):
-            f_ref[1 + x, c] = body_ref[x, c].astype(jnp.float32)
+            for z in range(nz):
+                f_ref[1 + x, z, c, :tall] = body_ref[x, c, z].astype(jnp.float32)
         return 0
     lax.fori_loop(0, nc, cast, 0)
     for c in range(nc):
         for z in range(nz):
-            f_ref[0, c, z] = halo(c, z).astype(jnp.float32)
+            f_ref[0, z, c, :tall] = halo(c, z).astype(jnp.float32)
     for z in range(nz):
         for x in range(2):
             decode(1 + x, z, body_ref[x, nc, z], body_ref[x, nc + 1, z])
         decode(0, z, halo(nc, z), halo(nc + 1, z))
 
+    def zero(c, _):
+        gf_ref[c] = jnp.zeros(gf_ref.shape[1:], jnp.float32)
+        gb_ref[c] = jnp.zeros(gb_ref.shape[1:], jnp.float32)
+        return 0
+    lax.fori_loop(0, nc, zero, 0)
+
     rows = lax.broadcasted_iota(jnp.int32, (256, 256), 0)
     cols = lax.broadcasted_iota(jnp.int32, (256, 256), 1)
 
-    def zero(i, _):
-        g_ref[i] = jnp.zeros(g_ref.shape[1:], jnp.float32)
-        return 0
-    lax.fori_loop(0, nc, zero, 0)
-
-    def pair(k, _):
+    def pair(k, acc_f, acc_b):
         oz, oy, ox = off_ref[k, 0], off_ref[k, 1], off_ref[k, 2]
         bit = jnp.left_shift(1, k)
         lo = jnp.maximum(0, -oz)
         hi = jnp.minimum(nz, nz - oz)
-
-        def shifted(slot, dx):
-            w_ref[slot] = jnp.where(rows == ((cols + dx) & 255), 1.0, 0.0).astype(jnp.bfloat16)
-            in0 = lane < dx
-            in1 = lane >= 128 + dx
-            def merge(h, a, b):
-                return jnp.concatenate([jnp.where(in0, h, a), jnp.where(in1, h, b)], axis=1)
-            return merge
-        merge_f = shifted(0, ox)
-        merge_b = shifted(1, -ox)
+        steps = tiles // 2
+
+        def columns(dx):
+            edge = jnp.where(dx > 0, 1, 2)
+            flip = jnp.where(dx > 0, 0, 128)
+            weight = jnp.where(rows == (((cols + dx) & 255) ^ flip), 1.0, 0.0).astype(jnp.bfloat16)
+            spill = (lane < dx) | (lane >= 128 + dx)
+            def merge(read):
+                return jnp.concatenate([jnp.where(spill, read(0), read(edge)), read(3 - edge)], axis=1)
+            return weight, merge
+        weight_f, merge_f = columns(ox)
+        weight_b, merge_b = columns(-ox)
 
         def label(z, r0, blk):
             m = m_ref[blk, z, pl.ds(r0, 8), :]
             t = t_ref[blk, z, pl.ds(r0, 8), :]
             return jnp.where((t & bit) != 0, -m, m)
 
-        def tile(t, own, src, dy, merge, slot, back):
-            r0 = 32 + dy + t * 8
-            parts = [merge(*(f_ref[blk, c, src, pl.ds(r0, 8), :] for blk in range(3))) for c in range(nc)]
-            if back:
-                lab = merge(*(label(src, r0, blk) for blk in range(3)))
-                parts += [lab, lab]
-            lhs = jnp.concatenate(parts, axis=0).astype(jnp.bfloat16)
-            p = jnp.dot(lhs, w_ref[slot], preferred_element_type=jnp.float32)
-            o0 = 32 + t * 8
+        def issue_f(acc, z, t, load=None):
+            r0 = 32 + oy + t * 8
+            parts = [merge_f(lambda blk: f_ref[blk, z + oz, c, pl.ds(r0, 8), :]) for c in range(nc)]
+            pltpu.matmul_acc_lhs(acc, jnp.concatenate(parts, axis=0).astype(jnp.bfloat16), load_staged_rhs=load)
+
+        def issue_b(acc, z, t, load=None):
+            r0 = 32 - oy + t * 8
+            parts = [merge_b(lambda blk: f_ref[blk, z, c, pl.ds(r0, 8), :]) for c in range(nc)]
+            lab = merge_b(lambda blk: label(z, r0, blk))
+            pltpu.matmul_acc_lhs(acc, jnp.concatenate(parts + [lab, lab], axis=0).astype(jnp.bfloat16), load_staged_rhs=load)
+
+        def consume(acc, g_ref, own, t, back):
+            p = pltpu.matmul_pop(acc)
+            o0 = pl.multiple_of(32 + t * 8, 8)
+            g0 = pl.multiple_of(own * 64 + t * 8, 8)
             for x in range(2):
                 xs = slice(x * 128, x * 128 + 128)
                 q = [p[c * 8:c * 8 + 8, xs] for c in range(nc)]
-                prods = [q[c] * f_ref[1 + x, c, own, o0:o0 + 8, :] for c in range(nc)]
+                prods = [q[c] * f_ref[1 + x, own, c, pl.ds(o0, 8), :] for c in range(nc)]
                 while len(prods) > 1:
                     prods = [u + v for u, v in zip(prods[::2], prods[1::2])]
                 if back:
@@ -218,24 +227,48 @@
                     keep = jnp.abs(lab)
                 else:
                     lab = label(own, o0, 1 + x)
-                    keep = m_ref[1 + x, own, o0:o0 + 8, :]
+                    keep = m_ref[1 + x, own, pl.ds(o0, 8), :]
                 s = keep * jnp.tanh(prods[0] * 0.5) + lab
                 for c in range(nc):
-                    g_ref[c, own, t * 8:t * 8 + 8, xs] += s * q[c]
-
-        def plane(z, _):
-            for t in range(0, tiles, per):
-                for i in range(t, t + per):
-                    tile(i, z, z + oz, oy, merge_f, 0, False)
-                for i in range(t, t + per):
-                    tile(i, z + oz, z, -oy, merge_b, 1, True)
+                    g_ref[c, x, pl.ds(g0, 8), :] += s * q[c]
+
+        pltpu.matmul_push_rhs(weight_f, 0, 0)
+        pltpu.matmul_push_rhs(weight_b, 0, 1)
+        issue_f(acc_f[0], lo, 0, 0)
+        issue_b(acc_b[0], lo, 0, 0)
+        issue_f(acc_f[1], lo, 1)
+        issue_b(acc_b[1], lo, 1)
+
+        def step(i, _):
+            z = lo + lax.shift_right_logical(i, 2)
+            t = (i & 3) * 2
+            j = jnp.minimum(i + 1, (hi - lo) * steps - 1)
+            zn = lo + lax.shift_right_logical(j, 2)
+            tn = (j & 3) * 2
+            for u in range(2):
+                consume(acc_f[u], gf_ref, z, t + u, False)
+                issue_f(acc_f[u], zn, tn + u)
+                consume(acc_b[u], gb_ref, z + oz, t + u, True)
+                issue_b(acc_b[u], zn, tn + u)
             return 0
-        lax.fori_loop(lo, hi, plane, 0)
-        return 0
-    lax.fori_loop(0, off_ref.shape[0], pair, 0)
+        lax.fori_loop(0, (hi - lo) * steps, step, 0)
+        for acc in (*acc_f, *acc_b):
+            pltpu.matmul_pop(acc)
+
+    def sweep(f0, f1, b0, b1):
+        def each(k, _):
+            pair(k, (f0, f1), (b0, b1))
+            return 0
+        lax.fori_loop(0, off_ref.shape[0], each, 0)
+    forward = pltpu.ACC(0)((nc * 8, 256), jnp.float32)
+    backward = pltpu.ACC(1)((nc * 8 + 16, 256), jnp.float32)
+    pl.run_scoped(sweep, forward, forward, backward, backward)
 
     def half(i, _):
-        g_ref[i] = g_ref[i] * 0.5
+        for z in range(nz):
+            for x in range(2):
+                at = slice(z * 64, z * 64 + 64)
+                g_ref[i, z, :, x * 128:x * 128 + 128] = (gf_ref[i, x, at] + gb_ref[i, x, at]) * 0.5
         return 0
     lax.fori_loop(0, nc, half, 0)
 
@@ -243,17 +276,19 @@
 def affinity(off, body, side):
     _, planes, nz, tall, _ = body.shape
     nc = planes - 2
+    rows = tall - 2 * HALO
     V = pl.BlockSpec(memory_space=pltpu.VMEM)
     return pl.pallas_call(
-        functools.partial(affinity_kernel, per=8),
-        out_shape=jax.ShapeDtypeStruct((nc, nz, tall - 2 * HALO, 2 * LANES), jnp.float32),
+        affinity_kernel,
+        out_shape=jax.ShapeDtypeStruct((nc, nz, rows, 2 * LANES), jnp.float32),
         in_specs=[pl.BlockSpec(memory_space=pltpu.SMEM), V, V],
         out_specs=V,
         scratch_shapes=[
-            pltpu.VMEM((3, nc, nz, tall, LANES), jnp.float32),
+            pltpu.VMEM((3, nz, nc, tall + PAD, LANES), jnp.float32),
             pltpu.VMEM((3, nz, tall, LANES), jnp.int32),
             pltpu.VMEM((3, nz, tall, LANES), jnp.float32),
-            pltpu.VMEM((2, 256, 256), jnp.bfloat16),
+            pltpu.VMEM((nc, 2, nz * rows + PAD, LANES), jnp.float32),
+            pltpu.VMEM((nc, 2, nz * rows + PAD, LANES), jnp.float32),
         ],
         compiler_params=pltpu.CompilerParams(vmem_limit_bytes=VMEM_BYTES),
         name="affinity",

time: 98.5 us -> 94 us (0.954)
  Pallas kernels: 97 us -> 92.5 us
    pallas_call x1, Pallas kernels: 58.2 us -> 53.7 us  [affinity(): pl.pallas_call(affinity_kernel, out_shape=jax.ShapeDtypeStruct((nc, nz, r...]
where the time goes in v3:
time: 94 us; the launch traced here: 93.9 us
  Pallas kernels  92.5 us (98%)
  local copies, waits for them, and re-layouts  1.36 us (1%)
    pallas_call x1, Pallas kernels, affinity(): pl.pallas_call(affinity_kernel, out_shape=jax.ShapeDtypeStruct((nc, nz, r...  53.7 us
    pallas_call x1, Pallas kernels, exchange(): pl.pallas_call(exchange_kernel, out_shape=(jax.ShapeDtypeStruct((2, plane...  38.8 us

profile of v3, /device:TPU:0, one launch (start us, length us, event | category | flops | bytes accessed | tf_op | source)
XLA Modules:
  0.0 93.9 jit_solution(7541204541895650672)
XLA Ops:
  0.0 1.4 %copy.5.off_ref = s32[12,3]{1,0:T(8,128)} copy(s32[12,3]{0,1:T(4,128)} %param.5) | data formatting | bytes 288 | tf_op args[1]
  1.4 38.8 %exchange.1 = (bf16[2,18,6,128,128]{4,3,2,1,0:T(8,128)(2,1)}, bf16[2,27,128,128]{3,2,1,0:T(8,128)(2,1)}) custom-call(bf16[16,6,64,256]{3,2,1,0:T(8,128)(2,1)} %e_ref.1, s32[6,64,256]{2,1,0:T(8,128)} %t_ref.1, s32[6,64,256]{2,1,0:T(8,128)} %m_ref.1), custom_call_target="tpu_custom_call" | custom-call | tf_op jit(solution)/shard_map/exchange/pallas_call | solution.py:119
  40.2 53.7 %affinity.1 = f32[16,6,64,256]{3,2,1,0:T(8,128)} custom-call(s32[12,3]{1,0:T(8,128)} %copy.5.off_ref, bf16[2,18,6,128,128]{4,3,2,1,0:T(8,128)(2,1)} %get-tuple-element.7.body_ref, bf16[2,27,128,128]{3,2,1,0:T(8,128)(2,1)} %get-tuple-element.8.side_ref), custom_call_target="tpu_custom_call" | custom-call | tf_op jit(solution)/shard_map/affinity/pallas_call | solution.py:281

commit v4 on v3

--- a/solution.py
+++ b/solution.py
@@ -29,14 +29,9 @@
     mine, tail, head = pl.ds(HALO, rows), pl.ds(rows, HALO), pl.ds(HALO, HALO)
     top, bottom = pl.ds(0, HALO), pl.ds(HALO + rows, HALO)
 
-    own = [
-        pltpu.make_async_copy(
-            e_ref.at[:, :, :, pl.ds(x * LANES, LANES)], body_ref.at[x, pl.ds(0, channels), :, mine], copied.at[x]
-        )
-        for x in range(2)
-    ]
-    for copy in own:
-        copy.start()
+    inner, codes = pl.ds(0, channels), pl.ds(channels, 2)
+    own = pltpu.make_async_copy(e_ref, body_ref.at[inner, :, mine], copied)
+    own.start()
 
     barrier = pltpu.get_barrier_semaphore()
     for neighbour in (below, above, right, left):
@@ -51,25 +46,19 @@
         copy.start()
         return copy
 
-    inner = pl.ds(0, channels)
-    flights = []
-    for x in range(2):
-        cols = pl.ds(x * LANES, LANES)
-        flights.append(remote(x, e_ref.at[:, :, pl.ds(rows - HALO, HALO), cols], body_ref.at[x, inner, :, top], below))
-        flights.append(remote(2 + x, e_ref.at[:, :, pl.ds(0, HALO), cols], body_ref.at[x, inner, :, bottom], above))
+    flights = [
+        remote(0, e_ref.at[:, :, pl.ds(rows - HALO, HALO)], body_ref.at[inner, :, top], below),
+        remote(1, e_ref.at[:, :, pl.ds(0, HALO)], body_ref.at[inner, :, bottom], above),
+    ]
 
     for z in range(slices):
-        for x in range(2):
-            cols = slice(x * LANES, (x + 1) * LANES)
-            code = t_ref[z, :, cols] | jnp.left_shift(m_ref[z, :, cols], 12)
-            body_ref[x, channels, z, HALO:HALO + rows] = (code & (LOW - 1)).astype(jnp.float32).astype(jnp.bfloat16)
-            body_ref[x, channels + 1, z, HALO:HALO + rows] = jnp.right_shift(code, 6).astype(jnp.float32).astype(jnp.bfloat16)
-    codes = pl.ds(channels, 2)
-    flights.append(remote(4, body_ref.at[:, codes, :, tail], body_ref.at[:, codes, :, top], below))
-    flights.append(remote(5, body_ref.at[:, codes, :, head], body_ref.at[:, codes, :, bottom], above))
-
-    for copy in own:
-        copy.wait()
+        code = t_ref[z] | jnp.left_shift(m_ref[z], 12)
+        body_ref[channels, z, HALO:HALO + rows] = (code & (LOW - 1)).astype(jnp.float32).astype(jnp.bfloat16)
+        body_ref[channels + 1, z, HALO:HALO + rows] = jnp.right_shift(code, 6).astype(jnp.float32).astype(jnp.bfloat16)
+    flights.append(remote(2, body_ref.at[codes, :, tail], body_ref.at[codes, :, top], below))
+    flights.append(remote(3, body_ref.at[codes, :, head], body_ref.at[codes, :, bottom], above))
+
+    own.wait()
     lane = lax.broadcasted_iota(jnp.int32, (rows, LANES), 1)
     across = []
     for x, device in ((1, right), (0, left)):
@@ -77,28 +66,29 @@
             packed = None
             for slot in range(SLOTS):
                 c, z = divmod(group * SLOTS + slot, slices)
-                moved = roll_to(body_ref[x, c, z, HALO:HALO + rows], x * (LANES - HALO), slot * HALO)
+                columns = body_ref[c, z, HALO:HALO + rows, x * LANES:(x + 1) * LANES]
+                moved = roll_to(columns, x * (LANES - HALO), slot * HALO)
                 packed = moved if packed is None else jnp.where(lane >= slot * HALO, moved, packed)
             strip_ref[x, group] = packed
-        across.append(remote(6 + x, strip_ref.at[x], side_ref.at[x, :, mine], device))
+        across.append(remote(4 + x, strip_ref.at[x], side_ref.at[x, :, mine], device))
     for copy in across:
         copy.wait()
 
     corners = [
-        remote(8, side_ref.at[:, :, tail], side_ref.at[:, :, top], below),
-        remote(9, side_ref.at[:, :, head], side_ref.at[:, :, bottom], above),
+        remote(6, side_ref.at[:, :, tail], side_ref.at[:, :, top], below),
+        remote(7, side_ref.at[:, :, head], side_ref.at[:, :, bottom], above),
     ]
     for copy in flights + corners:
         copy.wait()
 
     @pl.when(me_y == 0)
     def _():
-        body_ref[:, :, :, 0:HALO] = jnp.zeros((2, planes, slices, HALO, LANES), jnp.bfloat16)
+        body_ref[:, :, 0:HALO] = jnp.zeros((planes, slices, HALO, 2 * LANES), jnp.bfloat16)
         side_ref[:, :, 0:HALO] = jnp.zeros((2, groups, HALO, LANES), jnp.bfloat16)
 
     @pl.when(me_y == count_y - 1)
     def _():
-        body_ref[:, :, :, HALO + rows:] = jnp.zeros((2, planes, slices, HALO, LANES), jnp.bfloat16)
+        body_ref[:, :, HALO + rows:] = jnp.zeros((planes, slices, HALO, 2 * LANES), jnp.bfloat16)
         side_ref[:, :, HALO + rows:] = jnp.zeros((2, groups, HALO, LANES), jnp.bfloat16)
 
     @pl.when(me_x == 0)
@@ -119,16 +109,16 @@
     return pl.pallas_call(
         exchange_kernel,
         out_shape=(
-            jax.ShapeDtypeStruct((2, planes, slices, tall, LANES), jnp.bfloat16),
+            jax.ShapeDtypeStruct((planes, slices, tall, 2 * LANES), jnp.bfloat16),
             jax.ShapeDtypeStruct((2, groups, tall, LANES), jnp.bfloat16),
         ),
         in_specs=[pl.BlockSpec(memory_space=pl.ANY), V, V],
         out_specs=(V, V),
         scratch_shapes=[
             pltpu.VMEM((2, groups, rows, LANES), jnp.bfloat16),
-            pltpu.SemaphoreType.DMA((2,)),
-            pltpu.SemaphoreType.DMA((10,)),
-            pltpu.SemaphoreType.DMA((10,)),
+            pltpu.SemaphoreType.DMA,
+            pltpu.SemaphoreType.DMA((8,)),
+            pltpu.SemaphoreType.DMA((8,)),
         ],
         compiler_params=pltpu.CompilerParams(
             collective_id=0, has_side_effects=True, vmem_limit_bytes=VMEM_BYTES
@@ -137,12 +127,32 @@
     )(embedding, targets, mask)
 
 
-def affinity_kernel(off_ref, body_ref, side_ref, g_ref, f_ref, t_ref, m_ref, gf_ref, gb_ref):
-    _, planes, nz, tall, _ = body_ref.shape
+def affinity_kernel(off_ref, body_hbm, side_hbm, g_hbm, body_ref, side_ref, g_ref, f_ref, t_ref, m_ref, gf_ref, gb_ref,
+                    arrived, stored):
+    planes, nz, tall, _ = body_ref.shape
     nc = planes - 2
     tiles = (tall - 2 * HALO) // 8
     lane = lax.broadcasted_iota(jnp.int32, (8, 128), 1)
     wide = lax.broadcasted_iota(jnp.int32, (tall, LANES), 1)
+
+    def side_copy():
+        return pltpu.make_async_copy(side_hbm, side_ref, arrived.at[planes])
+
+    def plane_copy(c):
+        return pltpu.make_async_copy(body_hbm.at[c], body_ref.at[c], arrived.at[c])
+
+    def out_copy(c):
+        return pltpu.make_async_copy(g_ref.at[c], g_hbm.at[c], stored.at[c])
+
+    side_copy().start()
+    for c in range(planes):
+        plane_copy(c).start()
+
+    def zero(c, _):
+        gf_ref[c] = jnp.zeros(gf_ref.shape[1:], jnp.float32)
+        gb_ref[c] = jnp.zeros(gb_ref.shape[1:], jnp.float32)
+        return 0
+    lax.fori_loop(0, nc, zero, 0)
 
     def halo(c, z):
         group, slot = divmod(c * nz + z, SLOTS)
@@ -155,31 +165,30 @@
         t_ref[blk, z] = code
         m_ref[blk, z] = jnp.right_shift(code, 12).astype(jnp.float32)
 
-    def cast(c, _):
-        for x in range(2):
-            for z in range(nz):
-                f_ref[1 + x, z, c, :tall] = body_ref[x, c, z].astype(jnp.float32)
-        return 0
-    lax.fori_loop(0, nc, cast, 0)
+    side_copy().wait()
     for c in range(nc):
         for z in range(nz):
             f_ref[0, z, c, :tall] = halo(c, z).astype(jnp.float32)
+    def cast(c, _):
+        plane_copy(c).wait()
+        for x in range(2):
+            for z in range(nz):
+                f_ref[1 + x, z, c, :tall] = body_ref[c, z, :, x * LANES:(x + 1) * LANES].astype(jnp.float32)
+        return 0
+    lax.fori_loop(0, nc, cast, 0)
+    plane_copy(nc).wait()
+    plane_copy(nc + 1).wait()
     for z in range(nz):
         for x in range(2):
-            decode(1 + x, z, body_ref[x, nc, z], body_ref[x, nc + 1, z])
+            at = slice(x * LANES, (x + 1) * LANES)
+            decode(1 + x, z, body_ref[nc, z, :, at], body_ref[nc + 1, z, :, at])
         decode(0, z, halo(nc, z), halo(nc + 1, z))
-
-    def zero(c, _):
-        gf_ref[c] = jnp.zeros(gf_ref.shape[1:], jnp.float32)
-        gb_ref[c] = jnp.zeros(gb_ref.shape[1:], jnp.float32)
-        return 0
-    lax.fori_loop(0, nc, zero, 0)
 
     rows = lax.broadcasted_iota(jnp.int32, (256, 256), 0)
     cols = lax.broadcasted_iota(jnp.int32, (256, 256), 1)
 
     def pair(k, acc_f, acc_b):
-        oz, oy, ox = off_ref[k, 0], off_ref[k, 1], off_ref[k, 2]
+        oz, oy, ox = off_ref[0, k], off_ref[1, k], off_ref[2, k]
         bit = jnp.left_shift(1, k)
         lo = jnp.maximum(0, -oz)
         hi = jnp.minimum(nz, nz - oz)
@@ -259,7 +268,7 @@
         def each(k, _):
             pair(k, (f0, f1), (b0, b1))
             return 0
-        lax.fori_loop(0, off_ref.shape[0], each, 0)
+        lax.fori_loop(0, off_ref.shape[1], each, 0)
     forward = pltpu.ACC(0)((nc * 8, 256), jnp.float32)
     backward = pltpu.ACC(1)((nc * 8 + 16, 256), jnp.float32)
     pl.run_scoped(sweep, forward, forward, backward, backward)
@@ -269,26 +278,37 @@
             for x in range(2):
                 at = slice(z * 64, z * 64 + 64)
                 g_ref[i, z, :, x * 128:x * 128 + 128] = (gf_ref[i, x, at] + gb_ref[i, x, at]) * 0.5
+        out_copy(i).start()
         return 0
     lax.fori_loop(0, nc, half, 0)
 
+    def finish(i, _):
+        out_copy(i).wait()
+        return 0
+    lax.fori_loop(0, nc, finish, 0)
+
 
 def affinity(off, body, side):
-    _, planes, nz, tall, _ = body.shape
+    planes, nz, tall, _ = body.shape
     nc = planes - 2
     rows = tall - 2 * HALO
-    V = pl.BlockSpec(memory_space=pltpu.VMEM)
+    A = pl.BlockSpec(memory_space=pl.ANY)
     return pl.pallas_call(
         affinity_kernel,
         out_shape=jax.ShapeDtypeStruct((nc, nz, rows, 2 * LANES), jnp.float32),
-        in_specs=[pl.BlockSpec(memory_space=pltpu.SMEM), V, V],
-        out_specs=V,
+        in_specs=[pl.BlockSpec(memory_space=pltpu.SMEM), A, A],
+        out_specs=A,
         scratch_shapes=[
+            pltpu.VMEM(body.shape, body.dtype),
+            pltpu.VMEM(side.shape, side.dtype),
+            pltpu.VMEM((nc, nz, rows, 2 * LANES), jnp.float32),
             pltpu.VMEM((3, nz, nc, tall + PAD, LANES), jnp.float32),
             pltpu.VMEM((3, nz, tall, LANES), jnp.int32),
             pltpu.VMEM((3, nz, tall, LANES), jnp.float32),
             pltpu.VMEM((nc, 2, nz * rows + PAD, LANES), jnp.float32),
             pltpu.VMEM((nc, 2, nz * rows + PAD, LANES), jnp.float32),
+            pltpu.SemaphoreType.DMA((planes + 1,)),
+            pltpu.SemaphoreType.DMA((nc,)),
         ],
         compiler_params=pltpu.CompilerParams(vmem_limit_bytes=VMEM_BYTES),
         name="affinity",
@@ -296,7 +316,7 @@
 
 
 def on_device(embedding, offsets, targets, mask):
-    return affinity(offsets, *exchange(embedding, targets, mask))
+    return affinity(offsets.T, *exchange(embedding, targets, mask))
 
 
 def solution(mesh):

time: 94 us -> 87.6 us (0.932)
  Pallas kernels: 92.5 us -> 87.4 us
  local copies, waits for them, and re-layouts: 1.36 us -> 0 us
    pallas_call x1, Pallas kernels: 53.7 us -> 48.8 us  [affinity(): pl.pallas_call(affinity_kernel, out_shape=jax.ShapeDtypeStruct((nc, nz, r...]
    unnamed x1 -> x0, local copies, waits for them, and re-layouts: 1.36 us -> none
where the time goes in v4:
time: 87.6 us; the launch traced here: 87.4 us
  Pallas kernels  87.4 us (100%)
    pallas_call x1, Pallas kernels, affinity(): pl.pallas_call(affinity_kernel, out_shape=jax.ShapeDtypeStruct((nc, nz, r...  48.8 us
    pallas_call x1, Pallas kernels, exchange(): pl.pallas_call(exchange_kernel, out_shape=(jax.ShapeDtypeStruct((planes,...  38.6 us

profile of v4, /device:TPU:0, one launch (start us, length us, event | category | flops | bytes accessed | tf_op | source)
XLA Modules:
  0.0 87.4 jit_solution(4710381421481980537)
XLA Ops:
  0.0 38.6 %exchange.1 = (bf16[18,6,128,256]{3,2,1,0:T(8,128)(2,1)}, bf16[2,27,128,128]{3,2,1,0:T(8,128)(2,1)}) custom-call(bf16[16,6,64,256]{3,2,1,0:T(8,128)(2,1)} %e_ref.1, s32[6,64,256]{2,1,0:T(8,128)} %t_ref.1, s32[6,64,256]{2,1,0:T(8,128)} %m_ref.1), custom_call_target="tpu_custom_call" | custom-call | tf_op jit(solution)/shard_map/exchange/pallas_call | solution.py:109
  38.6 48.8 %affinity.1 = f32[16,6,64,256]{3,2,1,0:T(8,128)} custom-call(s32[3,12]{1,0:T(4,128)} %bitcast.1, bf16[18,6,128,256]{3,2,1,0:T(8,128)(2,1)} %get-tuple-element.7.body_hbm, bf16[2,27,128,128]{3,2,1,0:T(8,128)(2,1)} %get-tuple-element.8.side_hbm), custom_call_target="tpu_custom_call" | custom-call | tf_op jit(solution)/shard_map/affinity/pallas_call | solution.py:296
